TPU v7x, 32 devices: a whole 2x2x4 slice. The times are simulated.
32 devices in a mesh: layer: 8 (over z, core), row: 4 (over y, x).
Axes of the slice: x: 2, y: 2, z: 4, core: 2. Of those that a mesh axis runs over, the one named last changes fastest.
Arguments:
- propagator: float32 [8, 16384, 6, 128], P('layer', 'row'), may hold values from -0.15625 to 0.15625
- col_blocks: int32 [8, 128, 6], P('layer', 'row'), may hold values from 0 to 127, as said below
- sources: bfloat16 [8, 8, 56, 16384], P(None, 'layer', None, 'row'), may hold values from -6 to 6
- incoming: bfloat16 [8, 56, 16384], P('layer', None, 'row'), may hold values from -6 to 6
Outputs:
- outgoing: bfloat16 [8, 8, 56, 16384], P(None, 'layer', None, 'row')
Inputs may be any that keep to these rules, and one draw needn't show every extreme that they name: col_blocks[l, r, k] differs from r by at most 32; slot 0 is r itself, slots 1 and 2 are r - 32 and r + 32 kept within 0 .. 127; entries of one row block may repeat.
All inputs are finite; a program needn't handle non-finite values.
Results may differ from a plain program's by a relative error of at most 0.0043.
Values may be sent and summed in bfloat16 or wider, within the bound.
No kernel may reach another device: no remote copies, remote signals or barrier semaphores. Data moves between devices by JAX's collectives and lax.ppermute only.
A program may use at most 64 MiB of HBM per device.

v0:
```python
import functools

import jax
import jax.numpy as jnp
from jax import lax
from jax.experimental import pallas as pl
from jax.experimental.pallas import tpu as pltpu
from jax.sharding import PartitionSpec as P

MIB = 1024 * 1024


def split_kernel(prop_ref, weights_ref):
    slots, _, blk = prop_ref.shape
    for k in range(slots):
        block = prop_ref[k].T
        high = block.astype(jnp.bfloat16)
        low = (block - high.astype(jnp.float32)).astype(jnp.bfloat16)
        weights_ref[0, k * blk:(k + 1) * blk, :blk] = high
        weights_ref[0, k * blk:(k + 1) * blk, blk:] = low


def split_weights(prop):
    slots, rows, blk = prop.shape
    return pl.pallas_call(
        split_kernel,
        grid=(rows // blk,),
        in_specs=[pl.BlockSpec((slots, blk, blk), lambda r: (0, r, 0))],
        out_specs=pl.BlockSpec((1, slots * blk, 2 * blk), lambda r: (r, 0, 0)),
        out_shape=jax.ShapeDtypeStruct((rows // blk, slots * blk, 2 * blk), jnp.bfloat16),
        name="split_weights",
    )(prop)


def tick_kernel(cols_ref, weights_ref, left_ref, own_ref, right_ref, source_ref, out_ref, window):
    width = own_ref.shape[1]
    row_blocks, depth, twice = weights_ref.shape
    blk = twice // 2
    slots = depth // blk
    window[:, :width] = left_ref[...]
    window[:, width:2 * width] = own_ref[...]
    window[:, 2 * width:] = right_ref[...]

    def step(r, carry):
        picked = []
        for k in range(slots):
            start = pl.multiple_of(cols_ref[r * slots + k] * blk, blk)
            picked.append(window[:, pl.ds(start, blk)])
        both = jnp.dot(jnp.concatenate(picked, axis=1), weights_ref[r], preferred_element_type=jnp.float32)
        here = pl.ds(pl.multiple_of(r * blk, blk), blk)
        total = both[:, :blk] + both[:, blk:] + source_ref[:, here].astype(jnp.float32)
        out_ref[:, here] = total.astype(out_ref.dtype)
        return carry

    lax.fori_loop(0, row_blocks, step, 0, unroll=4)


def apply_layer(cols, weights, left, own, right, source):
    shots, width = own.shape
    vmem = pl.BlockSpec(memory_space=pltpu.VMEM)
    return pl.pallas_call(
        tick_kernel,
        in_specs=[pl.BlockSpec(memory_space=pltpu.SMEM)] + [vmem] * 5,
        out_specs=vmem,
        out_shape=jax.ShapeDtypeStruct((shots, width), jnp.bfloat16),
        scratch_shapes=[pltpu.VMEM((shots, 3 * width), jnp.bfloat16)],
        compiler_params=pltpu.CompilerParams(vmem_limit_bytes=32 * MIB),
        cost_estimate=pl.CostEstimate(
            flops=2 * shots * weights.size, bytes_accessed=weights.size * 2, transcendentals=0
        ),
        name="apply_layer",
    )(cols, weights, left, own, right, source)


def hop(value, layers, rows, up, side):
    pairs = []
    for l in range(layers - up):
        for r in range(rows):
            if 0 <= r + side < rows:
                pairs.append((l * rows + r, (l + up) * rows + r + side))
    return lax.ppermute(value, ("layer", "row"), pairs)


def body(propagator, col_blocks, sources, incoming):
    _, row_count, slots, blk = propagator.shape
    ticks = sources.shape[0]
    layers = lax.axis_size("layer")
    rows = lax.axis_size("row")
    block_count = row_count // blk
    cols = (col_blocks[0] - (lax.axis_index("row") - 1) * block_count).reshape(-1)
    own = incoming[0]
    left = hop(own, layers, rows, 0, 1)
    right = hop(own, layers, rows, 0, -1)
    weights = split_weights(jnp.transpose(propagator[0], (1, 0, 2)))
    history = []
    for tick in range(ticks):
        produced = apply_layer(cols, weights, left, own, right, sources[tick, 0])
        history.append(produced)
        if tick + 1 < ticks:
            left = hop(produced, layers, rows, 1, 1)
            right = hop(produced, layers, rows, 1, -1)
            own = hop(produced, layers, rows, 1, 0)
    return jnp.stack(history)[:, None]


def solution(mesh):
    return jax.shard_map(
        body,
        mesh=mesh,
        in_specs=(
            P("layer", "row", None, None),
            P("layer", "row", None),
            P(None, "layer", None, "row"),
            P("layer", None, "row"),
        ),
        out_specs=P(None, "layer", None, "row"),
        check_vma=False,
    )
```

profile of v0, /device:TPU:11, one launch (start us, length us, event | category | flops | bytes accessed | tf_op | source)
XLA Modules:
  0.0 229.5 jit_solution(1108955071387053048)
XLA Ops:
  9.1 23.0 %split_weights.1.weights_ref = bf16[32,768,256]{2,1,0:T(8,128)(2,1)} custom-call(f32[6,4096,128]{2,1,0:T(8,128)} %bitcast.42), custom_call_target="tpu_custom_call" | custom-call | tf_op jit(solution)/shard_map/split_weights/pallas_call | solution.py:25
  32.3 4.6 %copy-done = bf16[32,768,256]{2,1,0:T(8,128)(2,1)S(1)} copy-done((bf16[32,768,256]{2,1,0:T(8,128)(2,1)S(1)}, bf16[32,768,256]{2,1,0:T(8,128)(2,1)}, u32[]{:S(2)}) %copy-start) | copy-done | bytes 12582936
  37.9 4.5 %apply_layer.8 = bf16[56,4096]{1,0:T(8,128)(2,1)S(1)} custom-call(s32[192]{0:T(256)S(1)} %sub.16.cols_ref, bf16[32,768,256]{2,1,0:T(8,128)(2,1)S(1)} %copy-done, bf16[56,4096]{1,0:T(8,128)(2,1)} %collective-permute-done.left_ref, bf16[56,4096]{1,0:T(8,128)(2,1)S(1)} %bitcast.41, bf16[56,4096]{1,0:T(8,128)(2,1)} %collective-permute-done.1.right_ref, ...), custom_call_target="tpu_custom_call" | custom-call | flops 704643072 | bytes 12582912 | tf_op jit(solution)/shard_map/apply_layer/pallas_call | solution.py:61
  42.4 5.3 %collective-permute-start.2 = (bf16[56,4096]{1,0:T(8,128)(2,1)S(1)}, bf16[56,4096]{1,0:T(8,128)(2,1)S(1)}, u32[]{:S(2)}, u32[]{:S(2)}) collective-permute-start(bf16[56,4096]{1,0:T(8,128)(2,1)S(1)} %apply_layer.8), channel_id=1, source_target_pairs={{0,5},{1,6},{2,7},{4,9},{5,10},{6,11},{8,13},{9,14},{10,15},{12,17... | collective-permute-start | bytes 1376264 | tf_op jit(solution)/shard_map/ppermute | solution.py:81
  53.2 4.2 %collective-permute-done.2.left_ref = bf16[56,4096]{1,0:T(8,128)(2,1)S(1)} collective-permute-done((bf16[56,4096]{1,0:T(8,128)(2,1)S(1)}, bf16[56,4096]{1,0:T(8,128)(2,1)S(1)}, u32[]{:S(2)}, u32[]{:S(2)}) %collective-permute-start.2) | collective-permute-done | bytes 458784 | tf_op jit(solution)/shard_map/ppermute | solution.py:81
  58.1 9.8 %collective-permute-done.4.right_ref = bf16[56,4096]{1,0:T(8,128)(2,1)S(1)} collective-permute-done((bf16[56,4096]{1,0:T(8,128)(2,1)S(1)}, bf16[56,4096]{1,0:T(8,128)(2,1)S(1)}, u32[]{:S(2)}, u32[]{:S(2)}) %collective-permute-start.4) | collective-permute-done | bytes 458784 | tf_op jit(solution)/shard_map/ppermute | solution.py:81
  67.9 3.8 %apply_layer.9 = bf16[56,4096]{1,0:T(8,128)(2,1)S(1)} custom-call(s32[192]{0:T(256)S(1)} %sub.16.cols_ref, bf16[32,768,256]{2,1,0:T(8,128)(2,1)S(1)} %copy-done, bf16[56,4096]{1,0:T(8,128)(2,1)S(1)} %collective-permute-done.2.left_ref, bf16[56,4096]{1,0:T(8,128)(2,1)S(1)} %collective-permute-done.3.own_ref, ...), custom_call_target="tpu_custom_call" | custom-call | flops 704643072 | bytes 12582912 | tf_op jit(solution)/shard_map/apply_layer/pallas_call | solution.py:61
  76.4 3.8 %collective-permute-start.7 = (bf16[56,4096]{1,0:T(8,128)(2,1)S(1)}, bf16[56,4096]{1,0:T(8,128)(2,1)S(1)}, u32[]{:S(2)}, u32[]{:S(2)}) collective-permute-start(bf16[56,4096]{1,0:T(8,128)(2,1)S(1)} %apply_layer.9), channel_id=1, source_target_pairs={{1,4},{2,5},{3,6},{5,8},{6,9},{7,10},{9,12},{10,13},{11,14},{13,16... | collective-permute-start | bytes 1376264 | tf_op jit(solution)/shard_map/ppermute | solution.py:81
  80.3 5.5 %collective-permute-done.5.left_ref = bf16[56,4096]{1,0:T(8,128)(2,1)S(1)} collective-permute-done((bf16[56,4096]{1,0:T(8,128)(2,1)S(1)}, bf16[56,4096]{1,0:T(8,128)(2,1)S(1)}, u32[]{:S(2)}, u32[]{:S(2)}) %collective-permute-start.5) | collective-permute-done | bytes 458784 | tf_op jit(solution)/shard_map/ppermute | solution.py:81
  85.8 6.8 %collective-permute-done.7.right_ref = bf16[56,4096]{1,0:T(8,128)(2,1)S(1)} collective-permute-done((bf16[56,4096]{1,0:T(8,128)(2,1)S(1)}, bf16[56,4096]{1,0:T(8,128)(2,1)S(1)}, u32[]{:S(2)}, u32[]{:S(2)}) %collective-permute-start.7) | collective-permute-done | bytes 458784 | tf_op jit(solution)/shard_map/ppermute | solution.py:81
  92.6 3.8 %apply_layer.10 = bf16[56,4096]{1,0:T(8,128)(2,1)S(1)} custom-call(s32[192]{0:T(256)S(1)} %sub.16.cols_ref, bf16[32,768,256]{2,1,0:T(8,128)(2,1)S(1)} %copy-done, bf16[56,4096]{1,0:T(8,128)(2,1)S(1)} %collective-permute-done.5.left_ref, bf16[56,4096]{1,0:T(8,128)(2,1)S(1)} %collective-permute-done.6.own_ref, ...), custom_call_target="tpu_custom_call" | custom-call | flops 704643072 | bytes 12582912 | tf_op jit(solution)/shard_map/apply_layer/pallas_call | solution.py:61
  99.0 4.9 %collective-permute-start.8 = (bf16[56,4096]{1,0:T(8,128)(2,1)S(1)}, bf16[56,4096]{1,0:T(8,128)(2,1)S(1)}, u32[]{:S(2)}, u32[]{:S(2)}) collective-permute-start(bf16[56,4096]{1,0:T(8,128)(2,1)S(1)} %apply_layer.10), channel_id=1, source_target_pairs={{0,5},{1,6},{2,7},{4,9},{5,10},{6,11},{8,13},{9,14},{10,15},{12,17... | collective-permute-start | bytes 1376264 | tf_op jit(solution)/shard_map/ppermute | solution.py:81
  103.9 3.7 %collective-permute-start.9 = (bf16[56,4096]{1,0:T(8,128)(2,1)S(1)}, bf16[56,4096]{1,0:T(8,128)(2,1)S(1)}, u32[]{:S(2)}, u32[]{:S(2)}) collective-permute-start(bf16[56,4096]{1,0:T(8,128)(2,1)S(1)} %apply_layer.10), channel_id=1, source_target_pairs={{0,4},{1,5},{2,6},{3,7},{4,8},{5,9},{6,10},{7,11},{8,12},{9,13},{1... | collective-permute-start | bytes 1376264 | tf_op jit(solution)/shard_map/ppermute | solution.py:81
  107.7 9.3 %collective-permute-done.10.right_ref = bf16[56,4096]{1,0:T(8,128)(2,1)S(1)} collective-permute-done((bf16[56,4096]{1,0:T(8,128)(2,1)S(1)}, bf16[56,4096]{1,0:T(8,128)(2,1)S(1)}, u32[]{:S(2)}, u32[]{:S(2)}) %collective-permute-start.10) | collective-permute-done | bytes 458784 | tf_op jit(solution)/shard_map/ppermute | solution.py:81
  117.0 3.8 %apply_layer.11 = bf16[56,4096]{1,0:T(8,128)(2,1)S(1)} custom-call(s32[192]{0:T(256)S(1)} %sub.16.cols_ref, bf16[32,768,256]{2,1,0:T(8,128)(2,1)S(1)} %copy-done, bf16[56,4096]{1,0:T(8,128)(2,1)S(1)} %collective-permute-done.8.left_ref, bf16[56,4096]{1,0:T(8,128)(2,1)S(1)} %collective-permute-done.9.own_ref, ...), custom_call_target="tpu_custom_call" | custom-call | flops 704643072 | bytes 12582912 | tf_op jit(solution)/shard_map/apply_layer/pallas_call | solution.py:61
  120.8 7.7 %collective-permute-start.11 = (bf16[56,4096]{1,0:T(8,128)(2,1)S(1)}, bf16[56,4096]{1,0:T(8,128)(2,1)S(1)}, u32[]{:S(2)}, u32[]{:S(2)}) collective-permute-start(bf16[56,4096]{1,0:T(8,128)(2,1)S(1)} %apply_layer.11), channel_id=1, source_target_pairs={{0,5},{1,6},{2,7},{4,9},{5,10},{6,11},{8,13},{9,14},{10,15},{12,17... | collective-permute-start | bytes 1376264 | tf_op jit(solution)/shard_map/ppermute | solution.py:81
  138.9 7.8 %collective-permute-done.13.right_ref = bf16[56,4096]{1,0:T(8,128)(2,1)S(1)} collective-permute-done((bf16[56,4096]{1,0:T(8,128)(2,1)S(1)}, bf16[56,4096]{1,0:T(8,128)(2,1)S(1)}, u32[]{:S(2)}, u32[]{:S(2)}) %collective-permute-start.13) | collective-permute-done | bytes 458784 | tf_op jit(solution)/shard_map/ppermute | solution.py:81
  146.7 3.8 %apply_layer.12 = bf16[56,4096]{1,0:T(8,128)(2,1)S(1)} custom-call(s32[192]{0:T(256)S(1)} %sub.16.cols_ref, bf16[32,768,256]{2,1,0:T(8,128)(2,1)S(1)} %copy-done, bf16[56,4096]{1,0:T(8,128)(2,1)S(1)} %collective-permute-done.11.left_ref, bf16[56,4096]{1,0:T(8,128)(2,1)S(1)} %collective-permute-done.12.own_ref, ...), custom_call_target="tpu_custom_call" | custom-call | flops 704643072 | bytes 12582912 | tf_op jit(solution)/shard_map/apply_layer/pallas_call | solution.py:61
  150.6 4.1 %collective-permute-start.14 = (bf16[56,4096]{1,0:T(8,128)(2,1)S(1)}, bf16[56,4096]{1,0:T(8,128)(2,1)S(1)}, u32[]{:S(2)}, u32[]{:S(2)}) collective-permute-start(bf16[56,4096]{1,0:T(8,128)(2,1)S(1)} %apply_layer.12), channel_id=1, source_target_pairs={{0,5},{1,6},{2,7},{4,9},{5,10},{6,11},{8,13},{9,14},{10,15},{12,17... | collective-permute-start | bytes 1376264 | tf_op jit(solution)/shard_map/ppermute | solution.py:81
  157.6 3.9 %collective-permute-start.16 = (bf16[56,4096]{1,0:T(8,128)(2,1)S(1)}, bf16[56,4096]{1,0:T(8,128)(2,1)S(1)}, u32[]{:S(2)}, u32[]{:S(2)}) collective-permute-start(bf16[56,4096]{1,0:T(8,128)(2,1)S(1)} %apply_layer.12), channel_id=1, source_target_pairs={{1,4},{2,5},{3,6},{5,8},{6,9},{7,10},{9,12},{10,13},{11,14},{13,16... | collective-permute-start | bytes 1376264 | tf_op jit(solution)/shard_map/ppermute | solution.py:81
  161.5 4.0 %collective-permute-done.14.left_ref = bf16[56,4096]{1,0:T(8,128)(2,1)S(1)} collective-permute-done((bf16[56,4096]{1,0:T(8,128)(2,1)S(1)}, bf16[56,4096]{1,0:T(8,128)(2,1)S(1)}, u32[]{:S(2)}, u32[]{:S(2)}) %collective-permute-start.14) | collective-permute-done | bytes 458784 | tf_op jit(solution)/shard_map/ppermute | solution.py:81
  165.6 7.6 %collective-permute-done.16.right_ref = bf16[56,4096]{1,0:T(8,128)(2,1)S(1)} collective-permute-done((bf16[56,4096]{1,0:T(8,128)(2,1)S(1)}, bf16[56,4096]{1,0:T(8,128)(2,1)S(1)}, u32[]{:S(2)}, u32[]{:S(2)}) %collective-permute-start.16) | collective-permute-done | bytes 458784 | tf_op jit(solution)/shard_map/ppermute | solution.py:81
  173.2 3.8 %apply_layer.13 = bf16[56,4096]{1,0:T(8,128)(2,1)S(1)} custom-call(s32[192]{0:T(256)S(1)} %sub.16.cols_ref, bf16[32,768,256]{2,1,0:T(8,128)(2,1)S(1)} %copy-done, bf16[56,4096]{1,0:T(8,128)(2,1)S(1)} %collective-permute-done.14.left_ref, bf16[56,4096]{1,0:T(8,128)(2,1)S(1)} %collective-permute-done.15.own_ref, ...), custom_call_target="tpu_custom_call" | custom-call | flops 704643072 | bytes 12582912 | tf_op jit(solution)/shard_map/apply_layer/pallas_call | solution.py:61
  180.1 3.9 %collective-permute-start.18 = (bf16[56,4096]{1,0:T(8,128)(2,1)S(1)}, bf16[56,4096]{1,0:T(8,128)(2,1)S(1)}, u32[]{:S(2)}, u32[]{:S(2)}) collective-permute-start(bf16[56,4096]{1,0:T(8,128)(2,1)S(1)} %apply_layer.13), channel_id=1, source_target_pairs={{0,4},{1,5},{2,6},{3,7},{4,8},{5,9},{6,10},{7,11},{8,12},{9,13},{1... | collective-permute-start | bytes 1376264 | tf_op jit(solution)/shard_map/ppermute | solution.py:81
  184.0 4.0 %collective-permute-start.19 = (bf16[56,4096]{1,0:T(8,128)(2,1)S(1)}, bf16[56,4096]{1,0:T(8,128)(2,1)S(1)}, u32[]{:S(2)}, u32[]{:S(2)}) collective-permute-start(bf16[56,4096]{1,0:T(8,128)(2,1)S(1)} %apply_layer.13), channel_id=1, source_target_pairs={{1,4},{2,5},{3,6},{5,8},{6,9},{7,10},{9,12},{10,13},{11,14},{13,16... | collective-permute-start | bytes 1376264 | tf_op jit(solution)/shard_map/ppermute | solution.py:81
  188.0 4.0 %collective-permute-done.17.left_ref = bf16[56,4096]{1,0:T(8,128)(2,1)S(1)} collective-permute-done((bf16[56,4096]{1,0:T(8,128)(2,1)S(1)}, bf16[56,4096]{1,0:T(8,128)(2,1)S(1)}, u32[]{:S(2)}, u32[]{:S(2)}) %collective-permute-start.17) | collective-permute-done | bytes 458784 | tf_op jit(solution)/shard_map/ppermute | solution.py:81
  192.1 6.3 %collective-permute-done.19.right_ref = bf16[56,4096]{1,0:T(8,128)(2,1)S(1)} collective-permute-done((bf16[56,4096]{1,0:T(8,128)(2,1)S(1)}, bf16[56,4096]{1,0:T(8,128)(2,1)S(1)}, u32[]{:S(2)}, u32[]{:S(2)}) %collective-permute-start.19) | collective-permute-done | bytes 458784 | tf_op jit(solution)/shard_map/ppermute | solution.py:81
  198.4 3.8 %apply_layer.14 = bf16[56,4096]{1,0:T(8,128)(2,1)S(1)} custom-call(s32[192]{0:T(256)S(1)} %sub.16.cols_ref, bf16[32,768,256]{2,1,0:T(8,128)(2,1)S(1)} %copy-done, bf16[56,4096]{1,0:T(8,128)(2,1)S(1)} %collective-permute-done.17.left_ref, bf16[56,4096]{1,0:T(8,128)(2,1)S(1)} %collective-permute-done.18.own_ref, ...), custom_call_target="tpu_custom_call" | custom-call | flops 704643072 | bytes 12582912 | tf_op jit(solution)/shard_map/apply_layer/pallas_call | solution.py:61
  205.3 4.1 %collective-permute-start.21 = (bf16[56,4096]{1,0:T(8,128)(2,1)S(1)}, bf16[56,4096]{1,0:T(8,128)(2,1)S(1)}, u32[]{:S(2)}, u32[]{:S(2)}) collective-permute-start(bf16[56,4096]{1,0:T(8,128)(2,1)S(1)} %apply_layer.14), channel_id=1, source_target_pairs={{0,4},{1,5},{2,6},{3,7},{4,8},{5,9},{6,10},{7,11},{8,12},{9,13},{1... | collective-permute-start | bytes 1376264 | tf_op jit(solution)/shard_map/ppermute | solution.py:81
  213.1 4.1 %collective-permute-done.20 = bf16[56,4096]{1,0:T(8,128)(2,1)S(1)} collective-permute-done((bf16[56,4096]{1,0:T(8,128)(2,1)S(1)}, bf16[56,4096]{1,0:T(8,128)(2,1)S(1)}, u32[]{:S(2)}, u32[]{:S(2)}) %collective-permute-start.20) | collective-permute-done | bytes 458784 | tf_op jit(solution)/shard_map/ppermute | solution.py:81
  217.2 6.5 %collective-permute-done.22 = bf16[56,4096]{1,0:T(8,128)(2,1)S(1)} collective-permute-done((bf16[56,4096]{1,0:T(8,128)(2,1)S(1)}, bf16[56,4096]{1,0:T(8,128)(2,1)S(1)}, u32[]{:S(2)}, u32[]{:S(2)}) %collective-permute-start.22) | collective-permute-done | bytes 458784 | tf_op jit(solution)/shard_map/ppermute | solution.py:81
  223.8 3.9 %apply_layer.15 = bf16[8,56,4096]{2,1,0:T(8,128)(2,1)S(1)} fusion(bf16[8,56,4096]{2,1,0:T(8,128)(2,1)S(1)} %bitcast_dynamic-update-slice_fusion.1, s32[192]{0:T(256)S(1)} %sub.16.cols_ref, bf16[32,768,256]{2,1,0:T(8,128)(2,1)S(1)} %copy-done, bf16[56,4096]{1,0:T(8,128)(2,1)S(1)} %collective-permute-done.20, bf16[56,4096]{1,0:T(8,128)(2,1)S(1)} %collective-permute-done.21, ...), kind=kCustom, calls=%fused_computation | custom fusion | flops 704643072 | bytes 14877696 | tf_op jit(solution)/shard_map/apply_layer/pallas_call | solution.py:61
  (44 shorter events, 48.7 us)
Async XLA Ops:
  0.0 32.3 %collective-permute-start = (bf16[56,4096]{1,0:T(8,128)(2,1)}, bf16[56,4096]{1,0:T(8,128)(2,1)}, u32[]{:S(2)}, u32[]{:S(2)}) collective-permute-start(bf16[56,4096]{1,0:T(8,128)(2,1)} %bitcast.39), channel_id=1, source_target_pairs={{0,1},{1,2},{2,3},{4,5},{5,6},{6,7},{8,9},{9,10},{10,11},{12,13},{... | collective-permute-start | bytes 1376264 | tf_op jit(solution)/shard_map/ppermute | solution.py:81
  3.1 29.2 %collective-permute-start.1 = (bf16[56,4096]{1,0:T(8,128)(2,1)}, bf16[56,4096]{1,0:T(8,128)(2,1)}, u32[]{:S(2)}, u32[]{:S(2)}) collective-permute-start(bf16[56,4096]{1,0:T(8,128)(2,1)} %bitcast.40), channel_id=1, source_target_pairs={{1,0},{2,1},{3,2},{5,4},{6,5},{7,6},{9,8},{10,9},{11,10},{13,12},{... | collective-permute-start | bytes 1376264 | tf_op jit(solution)/shard_map/ppermute | solution.py:81
  9.1 23.0 %copy-start.4 = (s32[1,32,6]{1,0,2:T(1,128)S(1)}, s32[1,32,6]{1,0,2:T(1,128)}, u32[]{:S(2)}) copy-start(s32[1,32,6]{1,0,2:T(1,128)} %param.5) | copy-start | bytes 2308
  32.3 4.6 %copy-start = (bf16[32,768,256]{2,1,0:T(8,128)(2,1)S(1)}, bf16[32,768,256]{2,1,0:T(8,128)(2,1)}, u32[]{:S(2)}) copy-start(bf16[32,768,256]{2,1,0:T(8,128)(2,1)} %split_weights.1.weights_ref) | copy-start | bytes 37748740
  36.9 1.0 copy-start.1
  42.4 15.0 %collective-permute-start.2 = (bf16[56,4096]{1,0:T(8,128)(2,1)S(1)}, bf16[56,4096]{1,0:T(8,128)(2,1)S(1)}, u32[]{:S(2)}, u32[]{:S(2)}) collective-permute-start(bf16[56,4096]{1,0:T(8,128)(2,1)S(1)} %apply_layer.8), channel_id=1, source_target_pairs={{0,5},{1,6},{2,7},{4,9},{5,10},{6,11},{8,13},{9,14},{10,15},{12,17... | collective-permute-start | bytes 1376264 | tf_op jit(solution)/shard_map/ppermute | solution.py:81
  47.8 10.4 %collective-permute-start.3 = (bf16[56,4096]{1,0:T(8,128)(2,1)S(1)}, bf16[56,4096]{1,0:T(8,128)(2,1)S(1)}, u32[]{:S(2)}, u32[]{:S(2)}) collective-permute-start(bf16[56,4096]{1,0:T(8,128)(2,1)S(1)} %apply_layer.8), channel_id=1, source_target_pairs={{0,4},{1,5},{2,6},{3,7},{4,8},{5,9},{6,10},{7,11},{8,12},{9,13},{1... | collective-permute-start | bytes 1376264 | tf_op jit(solution)/shard_map/ppermute | solution.py:81
  49.7 18.2 %collective-permute-start.4 = (bf16[56,4096]{1,0:T(8,128)(2,1)S(1)}, bf16[56,4096]{1,0:T(8,128)(2,1)S(1)}, u32[]{:S(2)}, u32[]{:S(2)}) collective-permute-start(bf16[56,4096]{1,0:T(8,128)(2,1)S(1)} %apply_layer.8), channel_id=1, source_target_pairs={{1,4},{2,5},{3,6},{5,8},{6,9},{7,10},{9,12},{10,13},{11,14},{13,16... | collective-permute-start | bytes 1376264 | tf_op jit(solution)/shard_map/ppermute | solution.py:81
  71.7 14.1 %collective-permute-start.5 = (bf16[56,4096]{1,0:T(8,128)(2,1)S(1)}, bf16[56,4096]{1,0:T(8,128)(2,1)S(1)}, u32[]{:S(2)}, u32[]{:S(2)}) collective-permute-start(bf16[56,4096]{1,0:T(8,128)(2,1)S(1)} %apply_layer.9), channel_id=1, source_target_pairs={{0,5},{1,6},{2,7},{4,9},{5,10},{6,11},{8,13},{9,14},{10,15},{12,17... | collective-permute-start | bytes 1376264 | tf_op jit(solution)/shard_map/ppermute | solution.py:81
  74.5 11.3 %collective-permute-start.6 = (bf16[56,4096]{1,0:T(8,128)(2,1)S(1)}, bf16[56,4096]{1,0:T(8,128)(2,1)S(1)}, u32[]{:S(2)}, u32[]{:S(2)}) collective-permute-start(bf16[56,4096]{1,0:T(8,128)(2,1)S(1)} %apply_layer.9), channel_id=1, source_target_pairs={{0,4},{1,5},{2,6},{3,7},{4,8},{5,9},{6,10},{7,11},{8,12},{9,13},{1... | collective-permute-start | bytes 1376264 | tf_op jit(solution)/shard_map/ppermute | solution.py:81
  76.4 16.2 %collective-permute-start.7 = (bf16[56,4096]{1,0:T(8,128)(2,1)S(1)}, bf16[56,4096]{1,0:T(8,128)(2,1)S(1)}, u32[]{:S(2)}, u32[]{:S(2)}) collective-permute-start(bf16[56,4096]{1,0:T(8,128)(2,1)S(1)} %apply_layer.9), channel_id=1, source_target_pairs={{1,4},{2,5},{3,6},{5,8},{6,9},{7,10},{9,12},{10,13},{11,14},{13,16... | collective-permute-start | bytes 1376264 | tf_op jit(solution)/shard_map/ppermute | solution.py:81
  96.5 20.5 %collective-permute-start.10 = (bf16[56,4096]{1,0:T(8,128)(2,1)S(1)}, bf16[56,4096]{1,0:T(8,128)(2,1)S(1)}, u32[]{:S(2)}, u32[]{:S(2)}) collective-permute-start(bf16[56,4096]{1,0:T(8,128)(2,1)S(1)} %apply_layer.10), channel_id=1, source_target_pairs={{1,4},{2,5},{3,6},{5,8},{6,9},{7,10},{9,12},{10,13},{11,14},{13,16... | collective-permute-start | bytes 1376264 | tf_op jit(solution)/shard_map/ppermute | solution.py:81
  99.0 18.0 %collective-permute-start.8 = (bf16[56,4096]{1,0:T(8,128)(2,1)S(1)}, bf16[56,4096]{1,0:T(8,128)(2,1)S(1)}, u32[]{:S(2)}, u32[]{:S(2)}) collective-permute-start(bf16[56,4096]{1,0:T(8,128)(2,1)S(1)} %apply_layer.10), channel_id=1, source_target_pairs={{0,5},{1,6},{2,7},{4,9},{5,10},{6,11},{8,13},{9,14},{10,15},{12,17... | collective-permute-start | bytes 1376264 | tf_op jit(solution)/shard_map/ppermute | solution.py:81
  103.9 13.0 %collective-permute-start.9 = (bf16[56,4096]{1,0:T(8,128)(2,1)S(1)}, bf16[56,4096]{1,0:T(8,128)(2,1)S(1)}, u32[]{:S(2)}, u32[]{:S(2)}) collective-permute-start(bf16[56,4096]{1,0:T(8,128)(2,1)S(1)} %apply_layer.10), channel_id=1, source_target_pairs={{0,4},{1,5},{2,6},{3,7},{4,8},{5,9},{6,10},{7,11},{8,12},{9,13},{1... | collective-permute-start | bytes 1376264 | tf_op jit(solution)/shard_map/ppermute | solution.py:81
  120.8 15.0 %collective-permute-start.11 = (bf16[56,4096]{1,0:T(8,128)(2,1)S(1)}, bf16[56,4096]{1,0:T(8,128)(2,1)S(1)}, u32[]{:S(2)}, u32[]{:S(2)}) collective-permute-start(bf16[56,4096]{1,0:T(8,128)(2,1)S(1)} %apply_layer.11), channel_id=1, source_target_pairs={{0,5},{1,6},{2,7},{4,9},{5,10},{6,11},{8,13},{9,14},{10,15},{12,17... | collective-permute-start | bytes 1376264 | tf_op jit(solution)/shard_map/ppermute | solution.py:81
  128.5 10.4 %collective-permute-start.12 = (bf16[56,4096]{1,0:T(8,128)(2,1)S(1)}, bf16[56,4096]{1,0:T(8,128)(2,1)S(1)}, u32[]{:S(2)}, u32[]{:S(2)}) collective-permute-start(bf16[56,4096]{1,0:T(8,128)(2,1)S(1)} %apply_layer.11), channel_id=1, source_target_pairs={{0,4},{1,5},{2,6},{3,7},{4,8},{5,9},{6,10},{7,11},{8,12},{9,13},{1... | collective-permute-start | bytes 1376264 | tf_op jit(solution)/shard_map/ppermute | solution.py:81
  131.1 15.6 %collective-permute-start.13 = (bf16[56,4096]{1,0:T(8,128)(2,1)S(1)}, bf16[56,4096]{1,0:T(8,128)(2,1)S(1)}, u32[]{:S(2)}, u32[]{:S(2)}) collective-permute-start(bf16[56,4096]{1,0:T(8,128)(2,1)S(1)} %apply_layer.11), channel_id=1, source_target_pairs={{1,4},{2,5},{3,6},{5,8},{6,9},{7,10},{9,12},{10,13},{11,14},{13,16... | collective-permute-start | bytes 1376264 | tf_op jit(solution)/shard_map/ppermute | solution.py:81
  150.6 15.0 %collective-permute-start.14 = (bf16[56,4096]{1,0:T(8,128)(2,1)S(1)}, bf16[56,4096]{1,0:T(8,128)(2,1)S(1)}, u32[]{:S(2)}, u32[]{:S(2)}) collective-permute-start(bf16[56,4096]{1,0:T(8,128)(2,1)S(1)} %apply_layer.12), channel_id=1, source_target_pairs={{0,5},{1,6},{2,7},{4,9},{5,10},{6,11},{8,13},{9,14},{10,15},{12,17... | collective-permute-start | bytes 1376264 | tf_op jit(solution)/shard_map/ppermute | solution.py:81
  154.7 10.9 %collective-permute-start.15 = (bf16[56,4096]{1,0:T(8,128)(2,1)S(1)}, bf16[56,4096]{1,0:T(8,128)(2,1)S(1)}, u32[]{:S(2)}, u32[]{:S(2)}) collective-permute-start(bf16[56,4096]{1,0:T(8,128)(2,1)S(1)} %apply_layer.12), channel_id=1, source_target_pairs={{0,4},{1,5},{2,6},{3,7},{4,8},{5,9},{6,10},{7,11},{8,12},{9,13},{1... | collective-permute-start | bytes 1376264 | tf_op jit(solution)/shard_map/ppermute | solution.py:81
  157.6 15.6 %collective-permute-start.16 = (bf16[56,4096]{1,0:T(8,128)(2,1)S(1)}, bf16[56,4096]{1,0:T(8,128)(2,1)S(1)}, u32[]{:S(2)}, u32[]{:S(2)}) collective-permute-start(bf16[56,4096]{1,0:T(8,128)(2,1)S(1)} %apply_layer.12), channel_id=1, source_target_pairs={{1,4},{2,5},{3,6},{5,8},{6,9},{7,10},{9,12},{10,13},{11,14},{13,16... | collective-permute-start | bytes 1376264 | tf_op jit(solution)/shard_map/ppermute | solution.py:81
  177.1 15.0 %collective-permute-start.17 = (bf16[56,4096]{1,0:T(8,128)(2,1)S(1)}, bf16[56,4096]{1,0:T(8,128)(2,1)S(1)}, u32[]{:S(2)}, u32[]{:S(2)}) collective-permute-start(bf16[56,4096]{1,0:T(8,128)(2,1)S(1)} %apply_layer.13), channel_id=1, source_target_pairs={{0,5},{1,6},{2,7},{4,9},{5,10},{6,11},{8,13},{9,14},{10,15},{12,17... | collective-permute-start | bytes 1376264 | tf_op jit(solution)/shard_map/ppermute | solution.py:81
  180.1 11.9 %collective-permute-start.18 = (bf16[56,4096]{1,0:T(8,128)(2,1)S(1)}, bf16[56,4096]{1,0:T(8,128)(2,1)S(1)}, u32[]{:S(2)}, u32[]{:S(2)}) collective-permute-start(bf16[56,4096]{1,0:T(8,128)(2,1)S(1)} %apply_layer.13), channel_id=1, source_target_pairs={{0,4},{1,5},{2,6},{3,7},{4,8},{5,9},{6,10},{7,11},{8,12},{9,13},{1... | collective-permute-start | bytes 1376264 | tf_op jit(solution)/shard_map/ppermute | solution.py:81
  184.0 14.4 %collective-permute-start.19 = (bf16[56,4096]{1,0:T(8,128)(2,1)S(1)}, bf16[56,4096]{1,0:T(8,128)(2,1)S(1)}, u32[]{:S(2)}, u32[]{:S(2)}) collective-permute-start(bf16[56,4096]{1,0:T(8,128)(2,1)S(1)} %apply_layer.13), channel_id=1, source_target_pairs={{1,4},{2,5},{3,6},{5,8},{6,9},{7,10},{9,12},{10,13},{11,14},{13,16... | collective-permute-start | bytes 1376264 | tf_op jit(solution)/shard_map/ppermute | solution.py:81
  198.4 25.4 %copy-start.2 = (bf16[56,4096]{1,0:T(8,128)(2,1)S(1)}, bf16[56,4096]{1,0:T(8,128)(2,1)}, u32[]{:S(2)}) copy-start(bf16[56,4096]{1,0:T(8,128)(2,1)} %get-tuple-element.5) | copy-start | bytes 1376260
  202.2 15.0 %collective-permute-start.20 = (bf16[56,4096]{1,0:T(8,128)(2,1)S(1)}, bf16[56,4096]{1,0:T(8,128)(2,1)S(1)}, u32[]{:S(2)}, u32[]{:S(2)}) collective-permute-start(bf16[56,4096]{1,0:T(8,128)(2,1)S(1)} %apply_layer.14), channel_id=1, source_target_pairs={{0,5},{1,6},{2,7},{4,9},{5,10},{6,11},{8,13},{9,14},{10,15},{12,17... | collective-permute-start | bytes 1376264 | tf_op jit(solution)/shard_map/ppermute | solution.py:81
  205.3 12.0 %collective-permute-start.21 = (bf16[56,4096]{1,0:T(8,128)(2,1)S(1)}, bf16[56,4096]{1,0:T(8,128)(2,1)S(1)}, u32[]{:S(2)}, u32[]{:S(2)}) collective-permute-start(bf16[56,4096]{1,0:T(8,128)(2,1)S(1)} %apply_layer.14), channel_id=1, source_target_pairs={{0,4},{1,5},{2,6},{3,7},{4,8},{5,9},{6,10},{7,11},{8,12},{9,13},{1... | collective-permute-start | bytes 1376264 | tf_op jit(solution)/shard_map/ppermute | solution.py:81
  209.4 14.4 %collective-permute-start.22 = (bf16[56,4096]{1,0:T(8,128)(2,1)S(1)}, bf16[56,4096]{1,0:T(8,128)(2,1)S(1)}, u32[]{:S(2)}, u32[]{:S(2)}) collective-permute-start(bf16[56,4096]{1,0:T(8,128)(2,1)S(1)} %apply_layer.14), channel_id=1, source_target_pairs={{1,4},{2,5},{3,6},{5,8},{6,9},{7,10},{9,12},{10,13},{11,14},{13,16... | collective-permute-start | bytes 1376264 | tf_op jit(solution)/shard_map/ppermute | solution.py:81
  227.7 1.8 copy-start.3
where the time goes:
time: 234 us; the launch traced here: 229 us
  waiting for transfers between devices  82.5 us (35%)
  starting transfers between devices  81.4 us (35%)
  Pallas kernels  50.5 us (22%)
  local copies, waits for them, and re-layouts  10.9 us (5%)
  other arithmetic  3.87 us (2%)
    ppermute x23, waiting for transfers between devices, hop(): return lax.ppermute(value, ('layer', 'row'), pairs)  82.5 us
    ppermute x23, starting transfers between devices, hop(): return lax.ppermute(value, ('layer', 'row'), pairs)  81.4 us
    pallas_call x7, Pallas kernels, apply_layer(): pl.pallas_call(tick_kernel, in_specs=[pl.BlockSpec(memory_space=pltpu.SME...  27.5 us
    pallas_call x1, Pallas kernels, split_weights(): pl.pallas_call(split_kernel, grid=(rows // blk,), in_specs=[pl.BlockSpec(...  23 us
    unnamed x17, local copies, waits for them, and re-layouts  7.65 us
  transfers between devices with their start and end apart: 23, of which 15 were waited for; matrix products, arithmetic and copies ran while one was open for 2% of the time, Pallas kernels for 10%

commit v1 on v0

--- a/solution.py
+++ b/solution.py
@@ -10,24 +10,50 @@
 MIB = 1024 * 1024
 
 
-def split_kernel(prop_ref, weights_ref):
-    slots, _, blk = prop_ref.shape
-    for k in range(slots):
-        block = prop_ref[k].T
-        high = block.astype(jnp.bfloat16)
-        low = (block - high.astype(jnp.float32)).astype(jnp.bfloat16)
-        weights_ref[0, k * blk:(k + 1) * blk, :blk] = high
-        weights_ref[0, k * blk:(k + 1) * blk, blk:] = low
+def split_kernel(prop_ref, weights_ref, blocks, arrived):
+    row_blocks, depth, twice = weights_ref.shape
+    flight, slots, blk, _ = blocks.shape
+
+    def fetch(r, slot):
+        rows = pl.ds(pl.multiple_of(r * blk, blk), blk)
+        return pltpu.make_async_copy(prop_ref.at[:, rows, :], blocks.at[slot], arrived.at[slot])
+
+    for r in range(flight):
+        fetch(r, r).start()
+
+    def step(r, carry):
+        slot = lax.rem(r, flight)
+        fetch(r, slot).wait()
+        for k in range(slots):
+            block = blocks[slot, k].T
+            high = block.astype(jnp.bfloat16)
+            low = (block - high.astype(jnp.float32)).astype(jnp.bfloat16)
+            weights_ref[r, k * blk:(k + 1) * blk, :blk] = high
+            weights_ref[r, k * blk:(k + 1) * blk, blk:] = low
+
+        @pl.when(r + flight < row_blocks)
+        def _():
+            fetch(r + flight, slot).start()
+
+        return carry
+
+    lax.fori_loop(0, row_blocks, step, 0)
 
 
 def split_weights(prop):
     slots, rows, blk = prop.shape
+    flight = min(8, rows // blk)
     return pl.pallas_call(
         split_kernel,
-        grid=(rows // blk,),
-        in_specs=[pl.BlockSpec((slots, blk, blk), lambda r: (0, r, 0))],
-        out_specs=pl.BlockSpec((1, slots * blk, 2 * blk), lambda r: (r, 0, 0)),
+        in_specs=[pl.BlockSpec(memory_space=pl.ANY)],
+        out_specs=pl.BlockSpec(memory_space=pltpu.VMEM),
         out_shape=jax.ShapeDtypeStruct((rows // blk, slots * blk, 2 * blk), jnp.bfloat16),
+        scratch_shapes=[
+            pltpu.VMEM((flight, slots, blk, blk), jnp.float32),
+            pltpu.SemaphoreType.DMA((flight,)),
+        ],
+        compiler_params=pltpu.CompilerParams(vmem_limit_bytes=8 * MIB),
+        cost_estimate=pl.CostEstimate(flops=0, bytes_accessed=prop.size * 4, transcendentals=0),
         name="split_weights",
     )(prop)
 
@@ -64,7 +90,7 @@
         out_specs=vmem,
         out_shape=jax.ShapeDtypeStruct((shots, width), jnp.bfloat16),
         scratch_shapes=[pltpu.VMEM((shots, 3 * width), jnp.bfloat16)],
-        compiler_params=pltpu.CompilerParams(vmem_limit_bytes=32 * MIB),
+        compiler_params=pltpu.CompilerParams(vmem_limit_bytes=8 * MIB),
         cost_estimate=pl.CostEstimate(
             flops=2 * shots * weights.size, bytes_accessed=weights.size * 2, transcendentals=0
         ),
@@ -83,23 +109,27 @@
 
 def body(propagator, col_blocks, sources, incoming):
     _, row_count, slots, blk = propagator.shape
-    ticks = sources.shape[0]
+    ticks, _, shots, _ = sources.shape
     layers = lax.axis_size("layer")
     rows = lax.axis_size("row")
     block_count = row_count // blk
     cols = (col_blocks[0] - (lax.axis_index("row") - 1) * block_count).reshape(-1)
-    own = incoming[0]
-    left = hop(own, layers, rows, 0, 1)
-    right = hop(own, layers, rows, 0, -1)
+    cut = (shots // 16 + 1) // 2 * 16
+    panels = [(0, cut), (cut, shots)]
+    arriving = []
+    for a, b in panels:
+        own = incoming[0, a:b]
+        arriving.append((hop(own, layers, rows, 0, 1), own, hop(own, layers, rows, 0, -1)))
     weights = split_weights(jnp.transpose(propagator[0], (1, 0, 2)))
     history = []
     for tick in range(ticks):
-        produced = apply_layer(cols, weights, left, own, right, sources[tick, 0])
-        history.append(produced)
-        if tick + 1 < ticks:
-            left = hop(produced, layers, rows, 1, 1)
-            right = hop(produced, layers, rows, 1, -1)
-            own = hop(produced, layers, rows, 1, 0)
+        produced = []
+        for i, (a, b) in enumerate(panels):
+            done = apply_layer(cols, weights, *arriving[i], sources[tick, 0, a:b])
+            produced.append(done)
+            if tick + 1 < ticks:
+                arriving[i] = tuple(hop(done, layers, rows, 1, side) for side in (1, 0, -1))
+        history.append(jnp.concatenate(produced, axis=0))
     return jnp.stack(history)[:, None]
 
 

time: 234 us -> 224 us (0.957); the launches traced: 229 us -> 222 us
  waiting for transfers between devices: 82.5 us -> 23.9 us
  starting transfers between devices: 81.4 us -> 110 us
  Pallas kernels: 50.5 us -> 66 us
  local copies, waits for them, and re-layouts: 10.9 us -> 20.9 us
  other arithmetic: 3.87 us -> 0.28 us
    ppermute x23 -> x46, waiting for transfers between devices: 82.5 us -> 23.9 us  [hop(): return lax.ppermute(value, ('layer', 'row'), pairs)]
    pallas_call x7 -> x16, Pallas kernels: 27.5 us -> 58.9 us  [apply_layer(): pl.pallas_call(tick_kernel, in_specs=[pl.BlockSpec(memory_space=pltpu.SME...]
    ppermute x23 -> x46, starting transfers between devices: 81.4 us -> 110 us  [hop(): return lax.ppermute(value, ('layer', 'row'), pairs)]
    pallas_call x1, Pallas kernels: 23 us -> 7.09 us  [split_weights(): pl.pallas_call(split_kernel, in_specs=[pl.BlockSpec(memory_space=pl.ANY)]...]
    unnamed x17 -> x12, local copies, waits for them, and re-layouts: 7.65 us -> 15.5 us
    pallas_call x1 -> x0, other arithmetic: 3.87 us -> none  [apply_layer(): pl.pallas_call(tick_kernel, in_specs=[pl.BlockSpec(memory_space=pltpu.SME...]
    squeeze x1 -> x4, local copies, waits for them, and re-layouts: 3.05 us -> 5.12 us  [the longest x2 3.21 us: body(): done = apply_layer(cols, weights, *arriving[i], sources[tick, 0, a:b])]
  transfers between devices with their start and end apart: 23 -> 46, of which waited for: 15 -> 7; matrix products, arithmetic and copies ran while one was open for 2% -> 2% of each run, Pallas kernels for 10% -> 26%
where the time goes in v1:
time: 224 us; the launch traced here: 222 us
  starting transfers between devices  110 us (49%)
  Pallas kernels  66 us (29%)
  waiting for transfers between devices  23.9 us (11%)
  local copies, waits for them, and re-layouts  20.9 us (9%)
    ppermute x46, starting transfers between devices, hop(): return lax.ppermute(value, ('layer', 'row'), pairs)  110 us
    pallas_call x16, Pallas kernels, apply_layer(): pl.pallas_call(tick_kernel, in_specs=[pl.BlockSpec(memory_space=pltpu.SME...  58.9 us
    ppermute x46, waiting for transfers between devices, hop(): return lax.ppermute(value, ('layer', 'row'), pairs)  23.9 us
    unnamed x12, local copies, waits for them, and re-layouts  15.5 us
    pallas_call x1, Pallas kernels, split_weights(): pl.pallas_call(split_kernel, in_specs=[pl.BlockSpec(memory_space=pl.ANY)]...  7.09 us
  transfers between devices with their start and end apart: 46, of which 7 were waited for; matrix products, arithmetic and copies ran while one was open for 2% of the time, Pallas kernels for 26%

profile of v1, /device:TPU:11, one launch (start us, length us, event | category | flops | bytes accessed | tf_op | source)
XLA Modules:
  0.0 222.2 jit_solution(12022152288789654522)
XLA Ops:
  1.0 3.1 %collective-permute-start = (bf16[32,4096]{1,0:T(8,128)(2,1)S(1)}, bf16[32,4096]{1,0:T(8,128)(2,1)S(1)}, u32[]{:S(2)}, u32[]{:S(2)}) collective-permute-start(bf16[32,4096]{1,0:T(8,128)(2,1)S(1)} %slice_bitcast_fusion.8.own_ref), channel_id=1, source_target_pairs={{0,1},{1,2},{2,3},{4,5},{5,6},{6,7},{8,9},{9,10},{10,11},{12,13},{... | collective-permute-start | bytes 786440 | tf_op jit(solution)/shard_map/ppermute | solution.py:107
  7.2 4.0 %collective-permute-start.2 = (bf16[24,4096]{1,0:T(8,128)(2,1)S(1)}, bf16[24,4096]{1,0:T(8,128)(2,1)S(1)}, u32[]{:S(2)}, u32[]{:S(2)}) collective-permute-start(bf16[24,4096]{1,0:T(8,128)(2,1)S(1)} %slice_bitcast_fusion.17.own_ref), channel_id=1, source_target_pairs={{0,1},{1,2},{2,3},{4,5},{5,6},{6,7},{8,9},{9,10},{10,11},{12,13},{... | collective-permute-start | bytes 589832 | tf_op jit(solution)/shard_map/ppermute | solution.py:107
  13.2 4.6 %copy-done.3 = f32[1,4096,6,128]{3,1,2,0:T(8,128)S(1)} copy-done((f32[1,4096,6,128]{3,1,2,0:T(8,128)S(1)}, f32[1,4096,6,128]{3,1,2,0:T(8,128)}, u32[]{:S(2)}) %copy-start.3) | copy-done | bytes 12582936
  17.8 7.1 %split_weights.1.weights_ref = bf16[32,768,256]{2,1,0:T(8,128)(2,1)S(1)} custom-call(f32[6,4096,128]{2,1,0:T(8,128)S(1)} %bitcast.74), custom_call_target="tpu_custom_call" | custom-call | bytes 12582912 | tf_op jit(solution)/shard_map/split_weights/pallas_call | solution.py:46
  24.9 4.6 %copy-done = bf16[32,768,256]{2,1,0:T(8,128)(2,1)} copy-done((bf16[32,768,256]{2,1,0:T(8,128)(2,1)}, bf16[32,768,256]{2,1,0:T(8,128)(2,1)S(1)}, u32[]{:S(2)}) %copy-start) | copy-done | bytes 12582936
  31.2 4.6 %copy-done.1 = bf16[32,768,256]{2,1,0:T(8,128)(2,1)S(1)} copy-done((bf16[32,768,256]{2,1,0:T(8,128)(2,1)S(1)}, bf16[32,768,256]{2,1,0:T(8,128)(2,1)}, u32[]{:S(2)}) %copy-start.1) | copy-done | bytes 12582936
  35.8 3.7 %apply_layer.17 = bf16[24,4096]{1,0:T(8,128)(2,1)S(1)} custom-call(s32[192]{0:T(256)S(1)} %sub.16.cols_ref, bf16[32,768,256]{2,1,0:T(8,128)(2,1)S(1)} %copy-done.1, bf16[24,4096]{1,0:T(8,128)(2,1)S(1)} %collective-permute-done.2.left_ref, bf16[24,4096]{1,0:T(8,128)(2,1)S(1)} %slice_bitcast_fusion.17.own_ref, ...), custom_call_target="tpu_custom_call" | custom-call | flops 301989888 | bytes 12582912 | tf_op jit(solution)/shard_map/apply_layer/pallas_call | solution.py:87
  39.5 7.0 %collective-permute-start.7 = (bf16[24,4096]{1,0:T(8,128)(2,1)S(1)}, bf16[24,4096]{1,0:T(8,128)(2,1)S(1)}, u32[]{:S(2)}, u32[]{:S(2)}) collective-permute-start(bf16[24,4096]{1,0:T(8,128)(2,1)S(1)} %apply_layer.17), channel_id=1, source_target_pairs={{0,5},{1,6},{2,7},{4,9},{5,10},{6,11},{8,13},{9,14},{10,15},{12,17... | collective-permute-start | bytes 589832 | tf_op jit(solution)/shard_map/ppermute | solution.py:107
  48.1 3.7 %apply_layer.16 = bf16[32,4096]{1,0:T(8,128)(2,1)S(1)} custom-call(s32[192]{0:T(256)S(1)} %sub.16.cols_ref, bf16[32,768,256]{2,1,0:T(8,128)(2,1)S(1)} %copy-done.2, bf16[32,4096]{1,0:T(8,128)(2,1)S(1)} %collective-permute-done.left_ref, bf16[32,4096]{1,0:T(8,128)(2,1)S(1)} %slice_bitcast_fusion.8.own_ref, ...), custom_call_target="tpu_custom_call" | custom-call | flops 402653184 | bytes 12582912 | tf_op jit(solution)/shard_map/apply_layer/pallas_call | solution.py:87
  56.7 3.7 %collective-permute-start.9 = (bf16[24,4096]{1,0:T(8,128)(2,1)S(1)}, bf16[24,4096]{1,0:T(8,128)(2,1)S(1)}, u32[]{:S(2)}, u32[]{:S(2)}) collective-permute-start(bf16[24,4096]{1,0:T(8,128)(2,1)S(1)} %apply_layer.17), channel_id=1, source_target_pairs={{1,4},{2,5},{3,6},{5,8},{6,9},{7,10},{9,12},{10,13},{11,14},{13,16... | collective-permute-start | bytes 589832 | tf_op jit(solution)/shard_map/ppermute | solution.py:107
  66.4 3.7 %apply_layer.19 = bf16[24,4096]{1,0:T(8,128)(2,1)S(1)} custom-call(s32[192]{0:T(256)S(1)} %sub.16.cols_ref, bf16[32,768,256]{2,1,0:T(8,128)(2,1)S(1)} %copy-done.2, bf16[24,4096]{1,0:T(8,128)(2,1)S(1)} %collective-permute-done.7.left_ref, bf16[24,4096]{1,0:T(8,128)(2,1)S(1)} %collective-permute-done.8.own_ref, ...), custom_call_target="tpu_custom_call" | custom-call | flops 301989888 | bytes 12582912 | tf_op jit(solution)/shard_map/apply_layer/pallas_call | solution.py:87
  74.3 3.6 %collective-permute-start.15 = (bf16[24,4096]{1,0:T(8,128)(2,1)S(1)}, bf16[24,4096]{1,0:T(8,128)(2,1)S(1)}, u32[]{:S(2)}, u32[]{:S(2)}) collective-permute-start(bf16[24,4096]{1,0:T(8,128)(2,1)S(1)} %apply_layer.19), channel_id=1, source_target_pairs={{1,4},{2,5},{3,6},{5,8},{6,9},{7,10},{9,12},{10,13},{11,14},{13,16... | collective-permute-start | bytes 589832 | tf_op jit(solution)/shard_map/ppermute | solution.py:107
  77.9 3.7 %apply_layer.18 = bf16[32,4096]{1,0:T(8,128)(2,1)S(1)} custom-call(s32[192]{0:T(256)S(1)} %sub.16.cols_ref, bf16[32,768,256]{2,1,0:T(8,128)(2,1)S(1)} %copy-done.2, bf16[32,4096]{1,0:T(8,128)(2,1)S(1)} %collective-permute-done.4.left_ref, bf16[32,4096]{1,0:T(8,128)(2,1)S(1)} %collective-permute-done.5.own_ref, ...), custom_call_target="tpu_custom_call" | custom-call | flops 402653184 | bytes 12582912 | tf_op jit(solution)/shard_map/apply_layer/pallas_call | solution.py:87
  84.5 3.7 %apply_layer.21 = bf16[24,4096]{1,0:T(8,128)(2,1)S(1)} custom-call(s32[192]{0:T(256)S(1)} %sub.16.cols_ref, bf16[32,768,256]{2,1,0:T(8,128)(2,1)S(1)} %copy-done.2, bf16[24,4096]{1,0:T(8,128)(2,1)S(1)} %collective-permute-done.13.left_ref, bf16[24,4096]{1,0:T(8,128)(2,1)S(1)} %collective-permute-done.14.own_ref, ...), custom_call_target="tpu_custom_call" | custom-call | flops 301989888 | bytes 12582912 | tf_op jit(solution)/shard_map/apply_layer/pallas_call | solution.py:87
  92.0 3.4 %collective-permute-start.21 = (bf16[24,4096]{1,0:T(8,128)(2,1)S(1)}, bf16[24,4096]{1,0:T(8,128)(2,1)S(1)}, u32[]{:S(2)}, u32[]{:S(2)}) collective-permute-start(bf16[24,4096]{1,0:T(8,128)(2,1)S(1)} %apply_layer.21), channel_id=1, source_target_pairs={{1,4},{2,5},{3,6},{5,8},{6,9},{7,10},{9,12},{10,13},{11,14},{13,16... | collective-permute-start | bytes 589832 | tf_op jit(solution)/shard_map/ppermute | solution.py:107
  102.0 3.7 %apply_layer.23 = bf16[24,4096]{1,0:T(8,128)(2,1)S(1)} custom-call(s32[192]{0:T(256)S(1)} %sub.16.cols_ref, bf16[32,768,256]{2,1,0:T(8,128)(2,1)S(1)} %copy-done.2, bf16[24,4096]{1,0:T(8,128)(2,1)S(1)} %collective-permute-done.19.left_ref, bf16[24,4096]{1,0:T(8,128)(2,1)S(1)} %collective-permute-done.20.own_ref, ...), custom_call_target="tpu_custom_call" | custom-call | flops 301989888 | bytes 12582912 | tf_op jit(solution)/shard_map/apply_layer/pallas_call | solution.py:87
  109.5 3.4 %collective-permute-start.27 = (bf16[24,4096]{1,0:T(8,128)(2,1)S(1)}, bf16[24,4096]{1,0:T(8,128)(2,1)S(1)}, u32[]{:S(2)}, u32[]{:S(2)}) collective-permute-start(bf16[24,4096]{1,0:T(8,128)(2,1)S(1)} %apply_layer.23), channel_id=1, source_target_pairs={{1,4},{2,5},{3,6},{5,8},{6,9},{7,10},{9,12},{10,13},{11,14},{13,16... | collective-permute-start | bytes 589832 | tf_op jit(solution)/shard_map/ppermute | solution.py:107
  113.0 3.7 %apply_layer.20 = bf16[32,4096]{1,0:T(8,128)(2,1)S(1)} custom-call(s32[192]{0:T(256)S(1)} %sub.16.cols_ref, bf16[32,768,256]{2,1,0:T(8,128)(2,1)S(1)} %copy-done.2, bf16[32,4096]{1,0:T(8,128)(2,1)S(1)} %collective-permute-done.10.left_ref, bf16[32,4096]{1,0:T(8,128)(2,1)S(1)} %collective-permute-done.11.own_ref, ...), custom_call_target="tpu_custom_call" | custom-call | flops 402653184 | bytes 12582912 | tf_op jit(solution)/shard_map/apply_layer/pallas_call | solution.py:87
  123.4 3.7 %apply_layer.25 = bf16[24,4096]{1,0:T(8,128)(2,1)S(1)} custom-call(s32[192]{0:T(256)S(1)} %sub.16.cols_ref, bf16[32,768,256]{2,1,0:T(8,128)(2,1)S(1)} %copy-done.2, bf16[24,4096]{1,0:T(8,128)(2,1)S(1)} %collective-permute-done.25.left_ref, bf16[24,4096]{1,0:T(8,128)(2,1)S(1)} %collective-permute-done.26.own_ref, ...), custom_call_target="tpu_custom_call" | custom-call | flops 301989888 | bytes 12582912 | tf_op jit(solution)/shard_map/apply_layer/pallas_call | solution.py:87
  133.2 3.7 %apply_layer.22 = bf16[32,4096]{1,0:T(8,128)(2,1)S(1)} custom-call(s32[192]{0:T(256)S(1)} %sub.16.cols_ref, bf16[32,768,256]{2,1,0:T(8,128)(2,1)S(1)} %copy-done.2, bf16[32,4096]{1,0:T(8,128)(2,1)S(1)} %collective-permute-done.16.left_ref, bf16[32,4096]{1,0:T(8,128)(2,1)S(1)} %collective-permute-done.17.own_ref, ...), custom_call_target="tpu_custom_call" | custom-call | flops 402653184 | bytes 12582912 | tf_op jit(solution)/shard_map/apply_layer/pallas_call | solution.py:87
  141.5 3.8 %collective-permute-start.24 = (bf16[32,4096]{1,0:T(8,128)(2,1)S(1)}, bf16[32,4096]{1,0:T(8,128)(2,1)S(1)}, u32[]{:S(2)}, u32[]{:S(2)}) collective-permute-start(bf16[32,4096]{1,0:T(8,128)(2,1)S(1)} %apply_layer.22), channel_id=1, source_target_pairs={{1,4},{2,5},{3,6},{5,8},{6,9},{7,10},{9,12},{10,13},{11,14},{13,16... | collective-permute-start | bytes 786440 | tf_op jit(solution)/shard_map/ppermute | solution.py:107
  145.4 3.7 %apply_layer.27 = bf16[24,4096]{1,0:T(8,128)(2,1)S(1)} custom-call(s32[192]{0:T(256)S(1)} %sub.16.cols_ref, bf16[32,768,256]{2,1,0:T(8,128)(2,1)S(1)} %copy-done.2, bf16[24,4096]{1,0:T(8,128)(2,1)S(1)} %collective-permute-done.31.left_ref, bf16[24,4096]{1,0:T(8,128)(2,1)S(1)} %collective-permute-done.32.own_ref, ...), custom_call_target="tpu_custom_call" | custom-call | flops 301989888 | bytes 12582912 | tf_op jit(solution)/shard_map/apply_layer/pallas_call | solution.py:87
  155.8 3.7 %apply_layer.24 = bf16[32,4096]{1,0:T(8,128)(2,1)S(1)} custom-call(s32[192]{0:T(256)S(1)} %sub.16.cols_ref, bf16[32,768,256]{2,1,0:T(8,128)(2,1)S(1)} %copy-done.2, bf16[32,4096]{1,0:T(8,128)(2,1)S(1)} %collective-permute-done.22.left_ref, bf16[32,4096]{1,0:T(8,128)(2,1)S(1)} %collective-permute-done.23.own_ref, ...), custom_call_target="tpu_custom_call" | custom-call | flops 402653184 | bytes 12582912 | tf_op jit(solution)/shard_map/apply_layer/pallas_call | solution.py:87
  165.4 3.7 %apply_layer.29 = bf16[24,4096]{1,0:T(8,128)(2,1)S(1)} custom-call(s32[192]{0:T(256)S(1)} %sub.16.cols_ref, bf16[32,768,256]{2,1,0:T(8,128)(2,1)S(1)} %copy-done.2, bf16[24,4096]{1,0:T(8,128)(2,1)S(1)} %collective-permute-done.37.left_ref, bf16[24,4096]{1,0:T(8,128)(2,1)S(1)} %collective-permute-done.38.own_ref, ...), custom_call_target="tpu_custom_call" | custom-call | flops 301989888 | bytes 12582912 | tf_op jit(solution)/shard_map/apply_layer/pallas_call | solution.py:87
  175.1 3.5 %collective-permute-done.30.right_ref = bf16[32,4096]{1,0:T(8,128)(2,1)S(1)} collective-permute-done((bf16[32,4096]{1,0:T(8,128)(2,1)S(1)}, bf16[32,4096]{1,0:T(8,128)(2,1)S(1)}, u32[]{:S(2)}, u32[]{:S(2)}) %collective-permute-start.30) | collective-permute-done | bytes 262176 | tf_op jit(solution)/shard_map/ppermute | solution.py:107
  178.6 3.7 %apply_layer.26 = bf16[32,4096]{1,0:T(8,128)(2,1)S(1)} custom-call(s32[192]{0:T(256)S(1)} %sub.16.cols_ref, bf16[32,768,256]{2,1,0:T(8,128)(2,1)S(1)} %copy-done.2, bf16[32,4096]{1,0:T(8,128)(2,1)S(1)} %collective-permute-done.28.left_ref, bf16[32,4096]{1,0:T(8,128)(2,1)S(1)} %collective-permute-done.29.own_ref, ...), custom_call_target="tpu_custom_call" | custom-call | flops 402653184 | bytes 12582912 | tf_op jit(solution)/shard_map/apply_layer/pallas_call | solution.py:87
  188.2 3.7 %apply_layer.31 = bf16[24,4096]{1,0:T(8,128)(2,1)S(1)} custom-call(s32[192]{0:T(256)S(1)} %sub.16.cols_ref, bf16[32,768,256]{2,1,0:T(8,128)(2,1)S(1)} %copy-done.2, bf16[24,4096]{1,0:T(8,128)(2,1)S(1)} %collective-permute-done.43.left_ref, bf16[24,4096]{1,0:T(8,128)(2,1)S(1)} %collective-permute-done.44.own_ref, ...), custom_call_target="tpu_custom_call" | custom-call | flops 301989888 | bytes 12582912 | tf_op jit(solution)/shard_map/apply_layer/pallas_call | solution.py:87
  191.9 5.7 %collective-permute-done.36.right_ref = bf16[32,4096]{1,0:T(8,128)(2,1)S(1)} collective-permute-done((bf16[32,4096]{1,0:T(8,128)(2,1)S(1)}, bf16[32,4096]{1,0:T(8,128)(2,1)S(1)}, u32[]{:S(2)}, u32[]{:S(2)}) %collective-permute-start.36) | collective-permute-done | bytes 262176 | tf_op jit(solution)/shard_map/ppermute | solution.py:107
  197.6 3.7 %apply_layer.28 = bf16[32,4096]{1,0:T(8,128)(2,1)S(1)} custom-call(s32[192]{0:T(256)S(1)} %sub.16.cols_ref, bf16[32,768,256]{2,1,0:T(8,128)(2,1)S(1)} %copy-done.2, bf16[32,4096]{1,0:T(8,128)(2,1)S(1)} %collective-permute-done.34.left_ref, bf16[32,4096]{1,0:T(8,128)(2,1)S(1)} %collective-permute-done.35.own_ref, ...), custom_call_target="tpu_custom_call" | custom-call | flops 402653184 | bytes 12582912 | tf_op jit(solution)/shard_map/apply_layer/pallas_call | solution.py:87
  207.1 3.9 %collective-permute-done.40.left_ref = bf16[32,4096]{1,0:T(8,128)(2,1)S(1)} collective-permute-done((bf16[32,4096]{1,0:T(8,128)(2,1)S(1)}, bf16[32,4096]{1,0:T(8,128)(2,1)S(1)}, u32[]{:S(2)}, u32[]{:S(2)}) %collective-permute-start.40) | collective-permute-done | bytes 262176 | tf_op jit(solution)/shard_map/ppermute | solution.py:107
  211.0 5.6 %collective-permute-done.42.right_ref = bf16[32,4096]{1,0:T(8,128)(2,1)S(1)} collective-permute-done((bf16[32,4096]{1,0:T(8,128)(2,1)S(1)}, bf16[32,4096]{1,0:T(8,128)(2,1)S(1)}, u32[]{:S(2)}, u32[]{:S(2)}) %collective-permute-start.42) | collective-permute-done | bytes 262176 | tf_op jit(solution)/shard_map/ppermute | solution.py:107
  216.6 3.7 %apply_layer.30 = bf16[32,4096]{1,0:T(8,128)(2,1)S(1)} custom-call(s32[192]{0:T(256)S(1)} %sub.16.cols_ref, bf16[32,768,256]{2,1,0:T(8,128)(2,1)S(1)} %copy-done.2, bf16[32,4096]{1,0:T(8,128)(2,1)S(1)} %collective-permute-done.40.left_ref, bf16[32,4096]{1,0:T(8,128)(2,1)S(1)} %collective-permute-done.41.own_ref, ...), custom_call_target="tpu_custom_call" | custom-call | flops 402653184 | bytes 12582912 | tf_op jit(solution)/shard_map/apply_layer/pallas_call | solution.py:87
  (104 shorter events, 90.9 us)
Async XLA Ops:
  1.0 47.1 %collective-permute-start = (bf16[32,4096]{1,0:T(8,128)(2,1)S(1)}, bf16[32,4096]{1,0:T(8,128)(2,1)S(1)}, u32[]{:S(2)}, u32[]{:S(2)}) collective-permute-start(bf16[32,4096]{1,0:T(8,128)(2,1)S(1)} %slice_bitcast_fusion.8.own_ref), channel_id=1, source_target_pairs={{0,1},{1,2},{2,3},{4,5},{5,6},{6,7},{8,9},{9,10},{10,11},{12,13},{... | collective-permute-start | bytes 786440 | tf_op jit(solution)/shard_map/ppermute | solution.py:107
  4.1 44.0 %collective-permute-start.1 = (bf16[32,4096]{1,0:T(8,128)(2,1)S(1)}, bf16[32,4096]{1,0:T(8,128)(2,1)S(1)}, u32[]{:S(2)}, u32[]{:S(2)}) collective-permute-start(bf16[32,4096]{1,0:T(8,128)(2,1)S(1)} %slice_bitcast_fusion.8.own_ref), channel_id=1, source_target_pairs={{1,0},{2,1},{3,2},{5,4},{6,5},{7,6},{9,8},{10,9},{11,10},{13,12},{... | collective-permute-start | bytes 786440 | tf_op jit(solution)/shard_map/ppermute | solution.py:107
  7.2 24.0 %collective-permute-start.2 = (bf16[24,4096]{1,0:T(8,128)(2,1)S(1)}, bf16[24,4096]{1,0:T(8,128)(2,1)S(1)}, u32[]{:S(2)}, u32[]{:S(2)}) collective-permute-start(bf16[24,4096]{1,0:T(8,128)(2,1)S(1)} %slice_bitcast_fusion.17.own_ref), channel_id=1, source_target_pairs={{0,1},{1,2},{2,3},{4,5},{5,6},{6,7},{8,9},{9,10},{10,11},{12,13},{... | collective-permute-start | bytes 589832 | tf_op jit(solution)/shard_map/ppermute | solution.py:107
  11.2 20.0 %collective-permute-start.3 = (bf16[24,4096]{1,0:T(8,128)(2,1)S(1)}, bf16[24,4096]{1,0:T(8,128)(2,1)S(1)}, u32[]{:S(2)}, u32[]{:S(2)}) collective-permute-start(bf16[24,4096]{1,0:T(8,128)(2,1)S(1)} %slice_bitcast_fusion.17.own_ref), channel_id=1, source_target_pairs={{1,0},{2,1},{3,2},{5,4},{6,5},{7,6},{9,8},{10,9},{11,10},{13,12},{... | collective-permute-start | bytes 589832 | tf_op jit(solution)/shard_map/ppermute | solution.py:107
  39.5 22.8 %collective-permute-start.7 = (bf16[24,4096]{1,0:T(8,128)(2,1)S(1)}, bf16[24,4096]{1,0:T(8,128)(2,1)S(1)}, u32[]{:S(2)}, u32[]{:S(2)}) collective-permute-start(bf16[24,4096]{1,0:T(8,128)(2,1)S(1)} %apply_layer.17), channel_id=1, source_target_pairs={{0,5},{1,6},{2,7},{4,9},{5,10},{6,11},{8,13},{9,14},{10,15},{12,17... | collective-permute-start | bytes 589832 | tf_op jit(solution)/shard_map/ppermute | solution.py:107
  51.8 22.5 %collective-permute-start.4 = (bf16[32,4096]{1,0:T(8,128)(2,1)S(1)}, bf16[32,4096]{1,0:T(8,128)(2,1)S(1)}, u32[]{:S(2)}, u32[]{:S(2)}) collective-permute-start(bf16[32,4096]{1,0:T(8,128)(2,1)S(1)} %apply_layer.16), channel_id=1, source_target_pairs={{0,5},{1,6},{2,7},{4,9},{5,10},{6,11},{8,13},{9,14},{10,15},{12,17... | collective-permute-start | bytes 786440 | tf_op jit(solution)/shard_map/ppermute | solution.py:107
  60.4 17.5 %collective-permute-start.5 = (bf16[32,4096]{1,0:T(8,128)(2,1)S(1)}, bf16[32,4096]{1,0:T(8,128)(2,1)S(1)}, u32[]{:S(2)}, u32[]{:S(2)}) collective-permute-start(bf16[32,4096]{1,0:T(8,128)(2,1)S(1)} %apply_layer.16), channel_id=1, source_target_pairs={{0,4},{1,5},{2,6},{3,7},{4,8},{5,9},{6,10},{7,11},{8,12},{9,13},{1... | collective-permute-start | bytes 786440 | tf_op jit(solution)/shard_map/ppermute | solution.py:107
  62.3 15.6 %collective-permute-start.6 = (bf16[32,4096]{1,0:T(8,128)(2,1)S(1)}, bf16[32,4096]{1,0:T(8,128)(2,1)S(1)}, u32[]{:S(2)}, u32[]{:S(2)}) collective-permute-start(bf16[32,4096]{1,0:T(8,128)(2,1)S(1)} %apply_layer.16), channel_id=1, source_target_pairs={{1,4},{2,5},{3,6},{5,8},{6,9},{7,10},{9,12},{10,13},{11,14},{13,16... | collective-permute-start | bytes 786440 | tf_op jit(solution)/shard_map/ppermute | solution.py:107
  70.1 14.4 %collective-permute-start.13 = (bf16[24,4096]{1,0:T(8,128)(2,1)S(1)}, bf16[24,4096]{1,0:T(8,128)(2,1)S(1)}, u32[]{:S(2)}, u32[]{:S(2)}) collective-permute-start(bf16[24,4096]{1,0:T(8,128)(2,1)S(1)} %apply_layer.19), channel_id=1, source_target_pairs={{0,5},{1,6},{2,7},{4,9},{5,10},{6,11},{8,13},{9,14},{10,15},{12,17... | collective-permute-start | bytes 589832 | tf_op jit(solution)/shard_map/ppermute | solution.py:107
  72.1 12.3 %collective-permute-start.14 = (bf16[24,4096]{1,0:T(8,128)(2,1)S(1)}, bf16[24,4096]{1,0:T(8,128)(2,1)S(1)}, u32[]{:S(2)}, u32[]{:S(2)}) collective-permute-start(bf16[24,4096]{1,0:T(8,128)(2,1)S(1)} %apply_layer.19), channel_id=1, source_target_pairs={{0,4},{1,5},{2,6},{3,7},{4,8},{5,9},{6,10},{7,11},{8,12},{9,13},{1... | collective-permute-start | bytes 589832 | tf_op jit(solution)/shard_map/ppermute | solution.py:107
  81.6 27.9 %collective-permute-start.10 = (bf16[32,4096]{1,0:T(8,128)(2,1)S(1)}, bf16[32,4096]{1,0:T(8,128)(2,1)S(1)}, u32[]{:S(2)}, u32[]{:S(2)}) collective-permute-start(bf16[32,4096]{1,0:T(8,128)(2,1)S(1)} %apply_layer.18), channel_id=1, source_target_pairs={{0,5},{1,6},{2,7},{4,9},{5,10},{6,11},{8,13},{9,14},{10,15},{12,17... | collective-permute-start | bytes 786440 | tf_op jit(solution)/shard_map/ppermute | solution.py:107
  95.4 17.6 %collective-permute-start.11 = (bf16[32,4096]{1,0:T(8,128)(2,1)S(1)}, bf16[32,4096]{1,0:T(8,128)(2,1)S(1)}, u32[]{:S(2)}, u32[]{:S(2)}) collective-permute-start(bf16[32,4096]{1,0:T(8,128)(2,1)S(1)} %apply_layer.18), channel_id=1, source_target_pairs={{0,4},{1,5},{2,6},{3,7},{4,8},{5,9},{6,10},{7,11},{8,12},{9,13},{1... | collective-permute-start | bytes 786440 | tf_op jit(solution)/shard_map/ppermute | solution.py:107
  97.4 15.6 %collective-permute-start.12 = (bf16[32,4096]{1,0:T(8,128)(2,1)S(1)}, bf16[32,4096]{1,0:T(8,128)(2,1)S(1)}, u32[]{:S(2)}, u32[]{:S(2)}) collective-permute-start(bf16[32,4096]{1,0:T(8,128)(2,1)S(1)} %apply_layer.18), channel_id=1, source_target_pairs={{1,4},{2,5},{3,6},{5,8},{6,9},{7,10},{9,12},{10,13},{11,14},{13,16... | collective-permute-start | bytes 786440 | tf_op jit(solution)/shard_map/ppermute | solution.py:107
  105.7 15.8 %collective-permute-start.25 = (bf16[24,4096]{1,0:T(8,128)(2,1)S(1)}, bf16[24,4096]{1,0:T(8,128)(2,1)S(1)}, u32[]{:S(2)}, u32[]{:S(2)}) collective-permute-start(bf16[24,4096]{1,0:T(8,128)(2,1)S(1)} %apply_layer.23), channel_id=1, source_target_pairs={{0,5},{1,6},{2,7},{4,9},{5,10},{6,11},{8,13},{9,14},{10,15},{12,17... | collective-permute-start | bytes 589832 | tf_op jit(solution)/shard_map/ppermute | solution.py:107
  107.6 15.8 %collective-permute-start.26 = (bf16[24,4096]{1,0:T(8,128)(2,1)S(1)}, bf16[24,4096]{1,0:T(8,128)(2,1)S(1)}, u32[]{:S(2)}, u32[]{:S(2)}) collective-permute-start(bf16[24,4096]{1,0:T(8,128)(2,1)S(1)} %apply_layer.23), channel_id=1, source_target_pairs={{0,4},{1,5},{2,6},{3,7},{4,8},{5,9},{6,10},{7,11},{8,12},{9,13},{1... | collective-permute-start | bytes 589832 | tf_op jit(solution)/shard_map/ppermute | solution.py:107
  109.5 13.9 %collective-permute-start.27 = (bf16[24,4096]{1,0:T(8,128)(2,1)S(1)}, bf16[24,4096]{1,0:T(8,128)(2,1)S(1)}, u32[]{:S(2)}, u32[]{:S(2)}) collective-permute-start(bf16[24,4096]{1,0:T(8,128)(2,1)S(1)} %apply_layer.23), channel_id=1, source_target_pairs={{1,4},{2,5},{3,6},{5,8},{6,9},{7,10},{9,12},{10,13},{11,14},{13,16... | collective-permute-start | bytes 589832 | tf_op jit(solution)/shard_map/ppermute | solution.py:107
  116.7 14.3 %collective-permute-start.16 = (bf16[32,4096]{1,0:T(8,128)(2,1)S(1)}, bf16[32,4096]{1,0:T(8,128)(2,1)S(1)}, u32[]{:S(2)}, u32[]{:S(2)}) collective-permute-start(bf16[32,4096]{1,0:T(8,128)(2,1)S(1)} %apply_layer.20), channel_id=1, source_target_pairs={{0,5},{1,6},{2,7},{4,9},{5,10},{6,11},{8,13},{9,14},{10,15},{12,17... | collective-permute-start | bytes 786440 | tf_op jit(solution)/shard_map/ppermute | solution.py:107
  119.6 13.4 %collective-permute-start.17 = (bf16[32,4096]{1,0:T(8,128)(2,1)S(1)}, bf16[32,4096]{1,0:T(8,128)(2,1)S(1)}, u32[]{:S(2)}, u32[]{:S(2)}) collective-permute-start(bf16[32,4096]{1,0:T(8,128)(2,1)S(1)} %apply_layer.20), channel_id=1, source_target_pairs={{0,4},{1,5},{2,6},{3,7},{4,8},{5,9},{6,10},{7,11},{8,12},{9,13},{1... | collective-permute-start | bytes 786440 | tf_op jit(solution)/shard_map/ppermute | solution.py:107
  127.1 14.4 %collective-permute-start.31 = (bf16[24,4096]{1,0:T(8,128)(2,1)S(1)}, bf16[24,4096]{1,0:T(8,128)(2,1)S(1)}, u32[]{:S(2)}, u32[]{:S(2)}) collective-permute-start(bf16[24,4096]{1,0:T(8,128)(2,1)S(1)} %apply_layer.25), channel_id=1, source_target_pairs={{0,5},{1,6},{2,7},{4,9},{5,10},{6,11},{8,13},{9,14},{10,15},{12,17... | collective-permute-start | bytes 589832 | tf_op jit(solution)/shard_map/ppermute | solution.py:107
  129.1 16.3 %collective-permute-start.32 = (bf16[24,4096]{1,0:T(8,128)(2,1)S(1)}, bf16[24,4096]{1,0:T(8,128)(2,1)S(1)}, u32[]{:S(2)}, u32[]{:S(2)}) collective-permute-start(bf16[24,4096]{1,0:T(8,128)(2,1)S(1)} %apply_layer.25), channel_id=1, source_target_pairs={{0,4},{1,5},{2,6},{3,7},{4,8},{5,9},{6,10},{7,11},{8,12},{9,13},{1... | collective-permute-start | bytes 589832 | tf_op jit(solution)/shard_map/ppermute | solution.py:107
  131.0 14.4 %collective-permute-start.33 = (bf16[24,4096]{1,0:T(8,128)(2,1)S(1)}, bf16[24,4096]{1,0:T(8,128)(2,1)S(1)}, u32[]{:S(2)}, u32[]{:S(2)}) collective-permute-start(bf16[24,4096]{1,0:T(8,128)(2,1)S(1)} %apply_layer.25), channel_id=1, source_target_pairs={{1,4},{2,5},{3,6},{5,8},{6,9},{7,10},{9,12},{10,13},{11,14},{13,16... | collective-permute-start | bytes 589832 | tf_op jit(solution)/shard_map/ppermute | solution.py:107
  136.9 17.0 %collective-permute-start.22 = (bf16[32,4096]{1,0:T(8,128)(2,1)S(1)}, bf16[32,4096]{1,0:T(8,128)(2,1)S(1)}, u32[]{:S(2)}, u32[]{:S(2)}) collective-permute-start(bf16[32,4096]{1,0:T(8,128)(2,1)S(1)} %apply_layer.22), channel_id=1, source_target_pairs={{0,5},{1,6},{2,7},{4,9},{5,10},{6,11},{8,13},{9,14},{10,15},{12,17... | collective-permute-start | bytes 786440 | tf_op jit(solution)/shard_map/ppermute | solution.py:107
  139.6 16.2 %collective-permute-start.23 = (bf16[32,4096]{1,0:T(8,128)(2,1)S(1)}, bf16[32,4096]{1,0:T(8,128)(2,1)S(1)}, u32[]{:S(2)}, u32[]{:S(2)}) collective-permute-start(bf16[32,4096]{1,0:T(8,128)(2,1)S(1)} %apply_layer.22), channel_id=1, source_target_pairs={{0,4},{1,5},{2,6},{3,7},{4,8},{5,9},{6,10},{7,11},{8,12},{9,13},{1... | collective-permute-start | bytes 786440 | tf_op jit(solution)/shard_map/ppermute | solution.py:107
  141.5 14.3 %collective-permute-start.24 = (bf16[32,4096]{1,0:T(8,128)(2,1)S(1)}, bf16[32,4096]{1,0:T(8,128)(2,1)S(1)}, u32[]{:S(2)}, u32[]{:S(2)}) collective-permute-start(bf16[32,4096]{1,0:T(8,128)(2,1)S(1)} %apply_layer.22), channel_id=1, source_target_pairs={{1,4},{2,5},{3,6},{5,8},{6,9},{7,10},{9,12},{10,13},{11,14},{13,16... | collective-permute-start | bytes 786440 | tf_op jit(solution)/shard_map/ppermute | solution.py:107
  149.1 14.3 %collective-permute-start.37 = (bf16[24,4096]{1,0:T(8,128)(2,1)S(1)}, bf16[24,4096]{1,0:T(8,128)(2,1)S(1)}, u32[]{:S(2)}, u32[]{:S(2)}) collective-permute-start(bf16[24,4096]{1,0:T(8,128)(2,1)S(1)} %apply_layer.27), channel_id=1, source_target_pairs={{0,5},{1,6},{2,7},{4,9},{5,10},{6,11},{8,13},{9,14},{10,15},{12,17... | collective-permute-start | bytes 589832 | tf_op jit(solution)/shard_map/ppermute | solution.py:107
  151.9 13.4 %collective-permute-start.38 = (bf16[24,4096]{1,0:T(8,128)(2,1)S(1)}, bf16[24,4096]{1,0:T(8,128)(2,1)S(1)}, u32[]{:S(2)}, u32[]{:S(2)}) collective-permute-start(bf16[24,4096]{1,0:T(8,128)(2,1)S(1)} %apply_layer.27), channel_id=1, source_target_pairs={{0,4},{1,5},{2,6},{3,7},{4,8},{5,9},{6,10},{7,11},{8,12},{9,13},{1... | collective-permute-start | bytes 589832 | tf_op jit(solution)/shard_map/ppermute | solution.py:107
  159.5 13.6 %collective-permute-start.28 = (bf16[32,4096]{1,0:T(8,128)(2,1)S(1)}, bf16[32,4096]{1,0:T(8,128)(2,1)S(1)}, u32[]{:S(2)}, u32[]{:S(2)}) collective-permute-start(bf16[32,4096]{1,0:T(8,128)(2,1)S(1)} %apply_layer.24), channel_id=1, source_target_pairs={{0,5},{1,6},{2,7},{4,9},{5,10},{6,11},{8,13},{9,14},{10,15},{12,17... | collective-permute-start | bytes 786440 | tf_op jit(solution)/shard_map/ppermute | solution.py:107
  161.5 13.6 %collective-permute-start.29 = (bf16[32,4096]{1,0:T(8,128)(2,1)S(1)}, bf16[32,4096]{1,0:T(8,128)(2,1)S(1)}, u32[]{:S(2)}, u32[]{:S(2)}) collective-permute-start(bf16[32,4096]{1,0:T(8,128)(2,1)S(1)} %apply_layer.24), channel_id=1, source_target_pairs={{0,4},{1,5},{2,6},{3,7},{4,8},{5,9},{6,10},{7,11},{8,12},{9,13},{1... | collective-permute-start | bytes 786440 | tf_op jit(solution)/shard_map/ppermute | solution.py:107
  163.4 15.2 %collective-permute-start.30 = (bf16[32,4096]{1,0:T(8,128)(2,1)S(1)}, bf16[32,4096]{1,0:T(8,128)(2,1)S(1)}, u32[]{:S(2)}, u32[]{:S(2)}) collective-permute-start(bf16[32,4096]{1,0:T(8,128)(2,1)S(1)} %apply_layer.24), channel_id=1, source_target_pairs={{1,4},{2,5},{3,6},{5,8},{6,9},{7,10},{9,12},{10,13},{11,14},{13,16... | collective-permute-start | bytes 786440 | tf_op jit(solution)/shard_map/ppermute | solution.py:107
  169.0 17.2 %collective-permute-start.43 = (bf16[24,4096]{1,0:T(8,128)(2,1)S(1)}, bf16[24,4096]{1,0:T(8,128)(2,1)S(1)}, u32[]{:S(2)}, u32[]{:S(2)}) collective-permute-start(bf16[24,4096]{1,0:T(8,128)(2,1)S(1)} %apply_layer.29), channel_id=1, source_target_pairs={{0,5},{1,6},{2,7},{4,9},{5,10},{6,11},{8,13},{9,14},{10,15},{12,17... | collective-permute-start | bytes 589832 | tf_op jit(solution)/shard_map/ppermute | solution.py:107
  171.2 17.0 %collective-permute-start.44 = (bf16[24,4096]{1,0:T(8,128)(2,1)S(1)}, bf16[24,4096]{1,0:T(8,128)(2,1)S(1)}, u32[]{:S(2)}, u32[]{:S(2)}) collective-permute-start(bf16[24,4096]{1,0:T(8,128)(2,1)S(1)} %apply_layer.29), channel_id=1, source_target_pairs={{0,4},{1,5},{2,6},{3,7},{4,8},{5,9},{6,10},{7,11},{8,12},{9,13},{1... | collective-permute-start | bytes 589832 | tf_op jit(solution)/shard_map/ppermute | solution.py:107
  173.1 15.0 %collective-permute-start.45 = (bf16[24,4096]{1,0:T(8,128)(2,1)S(1)}, bf16[24,4096]{1,0:T(8,128)(2,1)S(1)}, u32[]{:S(2)}, u32[]{:S(2)}) collective-permute-start(bf16[24,4096]{1,0:T(8,128)(2,1)S(1)} %apply_layer.29), channel_id=1, source_target_pairs={{1,4},{2,5},{3,6},{5,8},{6,9},{7,10},{9,12},{10,13},{11,14},{13,16... | collective-permute-start | bytes 589832 | tf_op jit(solution)/shard_map/ppermute | solution.py:107
  (20 other events, 180.5 us)

commit v2 on v1

--- a/solution.py
+++ b/solution.py
@@ -10,8 +10,8 @@
 MIB = 1024 * 1024
 
 
-def split_kernel(prop_ref, weights_ref, blocks, arrived):
-    row_blocks, depth, twice = weights_ref.shape
+def convert_kernel(prop_ref, weights_ref, blocks, arrived):
+    row_blocks = weights_ref.shape[0]
     flight, slots, blk, _ = blocks.shape
 
     def fetch(r, slot):
@@ -25,11 +25,7 @@
         slot = lax.rem(r, flight)
         fetch(r, slot).wait()
         for k in range(slots):
-            block = blocks[slot, k].T
-            high = block.astype(jnp.bfloat16)
-            low = (block - high.astype(jnp.float32)).astype(jnp.bfloat16)
-            weights_ref[r, k * blk:(k + 1) * blk, :blk] = high
-            weights_ref[r, k * blk:(k + 1) * blk, blk:] = low
+            weights_ref[r, k * blk:(k + 1) * blk, :] = blocks[slot, k].astype(jnp.bfloat16).T
 
         @pl.when(r + flight < row_blocks)
         def _():
@@ -40,28 +36,27 @@
     lax.fori_loop(0, row_blocks, step, 0)
 
 
-def split_weights(prop):
+def convert_weights(prop):
     slots, rows, blk = prop.shape
     flight = min(8, rows // blk)
     return pl.pallas_call(
-        split_kernel,
-        in_specs=[pl.BlockSpec(memory_space=pl.ANY)],
+        convert_kernel,
+        in_specs=[pl.BlockSpec(memory_space=pltpu.HBM)],
         out_specs=pl.BlockSpec(memory_space=pltpu.VMEM),
-        out_shape=jax.ShapeDtypeStruct((rows // blk, slots * blk, 2 * blk), jnp.bfloat16),
+        out_shape=jax.ShapeDtypeStruct((rows // blk, slots * blk, blk), jnp.bfloat16),
         scratch_shapes=[
             pltpu.VMEM((flight, slots, blk, blk), jnp.float32),
             pltpu.SemaphoreType.DMA((flight,)),
         ],
-        compiler_params=pltpu.CompilerParams(vmem_limit_bytes=8 * MIB),
+        compiler_params=pltpu.CompilerParams(vmem_limit_bytes=48 * MIB),
         cost_estimate=pl.CostEstimate(flops=0, bytes_accessed=prop.size * 4, transcendentals=0),
-        name="split_weights",
+        name="convert_weights",
     )(prop)
 
 
 def tick_kernel(cols_ref, weights_ref, left_ref, own_ref, right_ref, source_ref, out_ref, window):
     width = own_ref.shape[1]
-    row_blocks, depth, twice = weights_ref.shape
-    blk = twice // 2
+    row_blocks, depth, blk = weights_ref.shape
     slots = depth // blk
     window[:, :width] = left_ref[...]
     window[:, width:2 * width] = own_ref[...]
@@ -72,13 +67,12 @@
         for k in range(slots):
             start = pl.multiple_of(cols_ref[r * slots + k] * blk, blk)
             picked.append(window[:, pl.ds(start, blk)])
-        both = jnp.dot(jnp.concatenate(picked, axis=1), weights_ref[r], preferred_element_type=jnp.float32)
+        mixed = jnp.dot(jnp.concatenate(picked, axis=1), weights_ref[r], preferred_element_type=jnp.float32)
         here = pl.ds(pl.multiple_of(r * blk, blk), blk)
-        total = both[:, :blk] + both[:, blk:] + source_ref[:, here].astype(jnp.float32)
-        out_ref[:, here] = total.astype(out_ref.dtype)
+        out_ref[:, here] = (mixed + source_ref[:, here].astype(jnp.float32)).astype(out_ref.dtype)
         return carry
 
-    lax.fori_loop(0, row_blocks, step, 0, unroll=4)
+    lax.fori_loop(0, row_blocks, step, 0, unroll=8)
 
 
 def apply_layer(cols, weights, left, own, right, source):
@@ -120,7 +114,7 @@
     for a, b in panels:
         own = incoming[0, a:b]
         arriving.append((hop(own, layers, rows, 0, 1), own, hop(own, layers, rows, 0, -1)))
-    weights = split_weights(jnp.transpose(propagator[0], (1, 0, 2)))
+    weights = convert_weights(jnp.transpose(propagator[0], (1, 0, 2)))
     history = []
     for tick in range(ticks):
         produced = []

time: 224 us -> 195 us (0.87)
  Pallas kernels: 66 us -> 41.2 us
  local copies, waits for them, and re-layouts: 20.9 us -> 9.94 us
  waiting for transfers between devices: 23.9 us -> 29.1 us
    pallas_call x16, Pallas kernels: 58.9 us -> 32.9 us  [apply_layer(): pl.pallas_call(tick_kernel, in_specs=[pl.BlockSpec(memory_space=pltpu.SME...]
    unnamed x12 -> x8, local copies, waits for them, and re-layouts: 15.5 us -> 4.63 us
    ppermute x46, waiting for transfers between devices: 23.9 us -> 29.1 us  [hop(): return lax.ppermute(value, ('layer', 'row'), pairs)]
  transfers between devices with their start and end apart: 46 -> 46, of which waited for: 7 -> 12; matrix products, arithmetic and copies ran while one was open for 2% -> 2% of each run, Pallas kernels for 26% -> 19%
where the time goes in v2:
time: 195 us; the launch traced here: 194 us
  starting transfers between devices  112 us (57%)
  Pallas kernels  41.2 us (21%)
  waiting for transfers between devices  29.1 us (15%)
  local copies, waits for them, and re-layouts  9.94 us (5%)
    ppermute x46, starting transfers between devices, hop(): return lax.ppermute(value, ('layer', 'row'), pairs)  112 us
    pallas_call x16, Pallas kernels, apply_layer(): pl.pallas_call(tick_kernel, in_specs=[pl.BlockSpec(memory_space=pltpu.SME...  32.9 us
    ppermute x46, waiting for transfers between devices, hop(): return lax.ppermute(value, ('layer', 'row'), pairs)  29.1 us
    pallas_call x1, Pallas kernels, convert_weights(): pl.pallas_call(convert_kernel, in_specs=[pl.BlockSpec(memory_space=pltpu....  8.29 us
    unnamed x8, local copies, waits for them, and re-layouts  4.63 us
  transfers between devices with their start and end apart: 46, of which 12 were waited for; matrix products, arithmetic and copies ran while one was open for 2% of the time, Pallas kernels for 19%

profile of v2, /device:TPU:11, one launch (start us, length us, event | category | flops | bytes accessed | tf_op | source)
XLA Modules:
  0.0 193.7 jit_solution(4955877842587658845)
XLA Ops:
  1.0 3.1 %collective-permute-start = (bf16[32,4096]{1,0:T(8,128)(2,1)S(1)}, bf16[32,4096]{1,0:T(8,128)(2,1)S(1)}, u32[]{:S(2)}, u32[]{:S(2)}) collective-permute-start(bf16[32,4096]{1,0:T(8,128)(2,1)S(1)} %slice_bitcast_fusion.8.own_ref), channel_id=1, source_target_pairs={{0,1},{1,2},{2,3},{4,5},{5,6},{6,7},{8,9},{9,10},{10,11},{12,13},{... | collective-permute-start | bytes 786440 | tf_op jit(solution)/shard_map/ppermute | solution.py:101
  4.1 2.2 %collective-permute-start.1 = (bf16[32,4096]{1,0:T(8,128)(2,1)S(1)}, bf16[32,4096]{1,0:T(8,128)(2,1)S(1)}, u32[]{:S(2)}, u32[]{:S(2)}) collective-permute-start(bf16[32,4096]{1,0:T(8,128)(2,1)S(1)} %slice_bitcast_fusion.8.own_ref), channel_id=1, source_target_pairs={{1,0},{2,1},{3,2},{5,4},{6,5},{7,6},{9,8},{10,9},{11,10},{13,12},{... | collective-permute-start | bytes 786440 | tf_op jit(solution)/shard_map/ppermute | solution.py:101
  7.2 4.0 %collective-permute-start.2 = (bf16[24,4096]{1,0:T(8,128)(2,1)S(1)}, bf16[24,4096]{1,0:T(8,128)(2,1)S(1)}, u32[]{:S(2)}, u32[]{:S(2)}) collective-permute-start(bf16[24,4096]{1,0:T(8,128)(2,1)S(1)} %slice_bitcast_fusion.17.own_ref), channel_id=1, source_target_pairs={{0,1},{1,2},{2,3},{4,5},{5,6},{6,7},{8,9},{9,10},{10,11},{12,13},{... | collective-permute-start | bytes 589832 | tf_op jit(solution)/shard_map/ppermute | solution.py:101
  13.2 8.3 %convert_weights.1.weights_ref = bf16[32,768,128]{2,1,0:T(8,128)(2,1)} custom-call(f32[6,4096,128]{2,1,0:T(8,128)} %bitcast.74), custom_call_target="tpu_custom_call" | custom-call | bytes 12582912 | tf_op jit(solution)/shard_map/convert_weights/pallas_call | solution.py:42
  25.0 2.8 %copy-done = bf16[32,768,128]{2,1,0:T(8,128)(2,1)S(1)} copy-done((bf16[32,768,128]{2,1,0:T(8,128)(2,1)S(1)}, bf16[32,768,128]{2,1,0:T(8,128)(2,1)}, u32[]{:S(2)}) %copy-start) | copy-done | bytes 6291480
  29.9 5.2 %collective-permute-start.7 = (bf16[24,4096]{1,0:T(8,128)(2,1)S(1)}, bf16[24,4096]{1,0:T(8,128)(2,1)S(1)}, u32[]{:S(2)}, u32[]{:S(2)}) collective-permute-start(bf16[24,4096]{1,0:T(8,128)(2,1)S(1)} %apply_layer.17), channel_id=1, source_target_pairs={{0,5},{1,6},{2,7},{4,9},{5,10},{6,11},{8,13},{9,14},{10,15},{12,17... | collective-permute-start | bytes 589832 | tf_op jit(solution)/shard_map/ppermute | solution.py:101
  36.8 2.1 %apply_layer.16 = bf16[32,4096]{1,0:T(8,128)(2,1)S(1)} custom-call(s32[192]{0:T(256)S(1)} %sub.16.cols_ref, bf16[32,768,128]{2,1,0:T(8,128)(2,1)S(1)} %copy-done.1, bf16[32,4096]{1,0:T(8,128)(2,1)S(1)} %collective-permute-done.left_ref, bf16[32,4096]{1,0:T(8,128)(2,1)S(1)} %slice_bitcast_fusion.8.own_ref, ...), custom_call_target="tpu_custom_call" | custom-call | flops 201326592 | bytes 6291456 | tf_op jit(solution)/shard_map/apply_layer/pallas_call | solution.py:81
  40.8 2.9 %collective-permute-start.8 = (bf16[24,4096]{1,0:T(8,128)(2,1)S(1)}, bf16[24,4096]{1,0:T(8,128)(2,1)S(1)}, u32[]{:S(2)}, u32[]{:S(2)}) collective-permute-start(bf16[24,4096]{1,0:T(8,128)(2,1)S(1)} %apply_layer.17), channel_id=1, source_target_pairs={{0,4},{1,5},{2,6},{3,7},{4,8},{5,9},{6,10},{7,11},{8,12},{9,13},{1... | collective-permute-start | bytes 589832 | tf_op jit(solution)/shard_map/ppermute | solution.py:101
  43.7 3.7 %collective-permute-start.9 = (bf16[24,4096]{1,0:T(8,128)(2,1)S(1)}, bf16[24,4096]{1,0:T(8,128)(2,1)S(1)}, u32[]{:S(2)}, u32[]{:S(2)}) collective-permute-start(bf16[24,4096]{1,0:T(8,128)(2,1)S(1)} %apply_layer.17), channel_id=1, source_target_pairs={{1,4},{2,5},{3,6},{5,8},{6,9},{7,10},{9,12},{10,13},{11,14},{13,16... | collective-permute-start | bytes 589832 | tf_op jit(solution)/shard_map/ppermute | solution.py:101
  51.2 2.2 %collective-permute-done.9.right_ref = bf16[24,4096]{1,0:T(8,128)(2,1)S(1)} collective-permute-done((bf16[24,4096]{1,0:T(8,128)(2,1)S(1)}, bf16[24,4096]{1,0:T(8,128)(2,1)S(1)}, u32[]{:S(2)}, u32[]{:S(2)}) %collective-permute-start.9) | collective-permute-done | bytes 196640 | tf_op jit(solution)/shard_map/ppermute | solution.py:101
  57.5 2.2 %collective-permute-start.14 = (bf16[24,4096]{1,0:T(8,128)(2,1)S(1)}, bf16[24,4096]{1,0:T(8,128)(2,1)S(1)}, u32[]{:S(2)}, u32[]{:S(2)}) collective-permute-start(bf16[24,4096]{1,0:T(8,128)(2,1)S(1)} %apply_layer.19), channel_id=1, source_target_pairs={{0,4},{1,5},{2,6},{3,7},{4,8},{5,9},{6,10},{7,11},{8,12},{9,13},{1... | collective-permute-start | bytes 589832 | tf_op jit(solution)/shard_map/ppermute | solution.py:101
  59.7 3.6 %collective-permute-start.15 = (bf16[24,4096]{1,0:T(8,128)(2,1)S(1)}, bf16[24,4096]{1,0:T(8,128)(2,1)S(1)}, u32[]{:S(2)}, u32[]{:S(2)}) collective-permute-start(bf16[24,4096]{1,0:T(8,128)(2,1)S(1)} %apply_layer.19), channel_id=1, source_target_pairs={{1,4},{2,5},{3,6},{5,8},{6,9},{7,10},{9,12},{10,13},{11,14},{13,16... | collective-permute-start | bytes 589832 | tf_op jit(solution)/shard_map/ppermute | solution.py:101
  63.3 2.1 %apply_layer.18 = bf16[32,4096]{1,0:T(8,128)(2,1)S(1)} custom-call(s32[192]{0:T(256)S(1)} %sub.16.cols_ref, bf16[32,768,128]{2,1,0:T(8,128)(2,1)S(1)} %copy-done.1, bf16[32,4096]{1,0:T(8,128)(2,1)S(1)} %collective-permute-done.4.left_ref, bf16[32,4096]{1,0:T(8,128)(2,1)S(1)} %collective-permute-done.5.own_ref, ...), custom_call_target="tpu_custom_call" | custom-call | flops 201326592 | bytes 6291456 | tf_op jit(solution)/shard_map/apply_layer/pallas_call | solution.py:81
  65.4 2.8 %collective-permute-start.10 = (bf16[32,4096]{1,0:T(8,128)(2,1)S(1)}, bf16[32,4096]{1,0:T(8,128)(2,1)S(1)}, u32[]{:S(2)}, u32[]{:S(2)}) collective-permute-start(bf16[32,4096]{1,0:T(8,128)(2,1)S(1)} %apply_layer.18), channel_id=1, source_target_pairs={{0,5},{1,6},{2,7},{4,9},{5,10},{6,11},{8,13},{9,14},{10,15},{12,17... | collective-permute-start | bytes 786440 | tf_op jit(solution)/shard_map/ppermute | solution.py:101
  75.6 3.6 %collective-permute-start.21 = (bf16[24,4096]{1,0:T(8,128)(2,1)S(1)}, bf16[24,4096]{1,0:T(8,128)(2,1)S(1)}, u32[]{:S(2)}, u32[]{:S(2)}) collective-permute-start(bf16[24,4096]{1,0:T(8,128)(2,1)S(1)} %apply_layer.21), channel_id=1, source_target_pairs={{1,4},{2,5},{3,6},{5,8},{6,9},{7,10},{9,12},{10,13},{11,14},{13,16... | collective-permute-start | bytes 589832 | tf_op jit(solution)/shard_map/ppermute | solution.py:101
  83.1 2.5 %collective-permute-done.21.right_ref = bf16[24,4096]{1,0:T(8,128)(2,1)S(1)} collective-permute-done((bf16[24,4096]{1,0:T(8,128)(2,1)S(1)}, bf16[24,4096]{1,0:T(8,128)(2,1)S(1)}, u32[]{:S(2)}, u32[]{:S(2)}) %collective-permute-start.21) | collective-permute-done | bytes 196640 | tf_op jit(solution)/shard_map/ppermute | solution.py:101
  91.5 3.6 %collective-permute-start.27 = (bf16[24,4096]{1,0:T(8,128)(2,1)S(1)}, bf16[24,4096]{1,0:T(8,128)(2,1)S(1)}, u32[]{:S(2)}, u32[]{:S(2)}) collective-permute-start(bf16[24,4096]{1,0:T(8,128)(2,1)S(1)} %apply_layer.23), channel_id=1, source_target_pairs={{1,4},{2,5},{3,6},{5,8},{6,9},{7,10},{9,12},{10,13},{11,14},{13,16... | collective-permute-start | bytes 589832 | tf_op jit(solution)/shard_map/ppermute | solution.py:101
  95.2 2.1 %apply_layer.20 = bf16[32,4096]{1,0:T(8,128)(2,1)S(1)} custom-call(s32[192]{0:T(256)S(1)} %sub.16.cols_ref, bf16[32,768,128]{2,1,0:T(8,128)(2,1)S(1)} %copy-done.1, bf16[32,4096]{1,0:T(8,128)(2,1)S(1)} %collective-permute-done.10.left_ref, bf16[32,4096]{1,0:T(8,128)(2,1)S(1)} %collective-permute-done.11.own_ref, ...), custom_call_target="tpu_custom_call" | custom-call | flops 201326592 | bytes 6291456 | tf_op jit(solution)/shard_map/apply_layer/pallas_call | solution.py:81
  97.3 2.8 %collective-permute-start.16 = (bf16[32,4096]{1,0:T(8,128)(2,1)S(1)}, bf16[32,4096]{1,0:T(8,128)(2,1)S(1)}, u32[]{:S(2)}, u32[]{:S(2)}) collective-permute-start(bf16[32,4096]{1,0:T(8,128)(2,1)S(1)} %apply_layer.20), channel_id=1, source_target_pairs={{0,5},{1,6},{2,7},{4,9},{5,10},{6,11},{8,13},{9,14},{10,15},{12,17... | collective-permute-start | bytes 786440 | tf_op jit(solution)/shard_map/ppermute | solution.py:101
  106.0 2.6 %collective-permute-start.31 = (bf16[24,4096]{1,0:T(8,128)(2,1)S(1)}, bf16[24,4096]{1,0:T(8,128)(2,1)S(1)}, u32[]{:S(2)}, u32[]{:S(2)}) collective-permute-start(bf16[24,4096]{1,0:T(8,128)(2,1)S(1)} %apply_layer.25), channel_id=1, source_target_pairs={{0,5},{1,6},{2,7},{4,9},{5,10},{6,11},{8,13},{9,14},{10,15},{12,17... | collective-permute-start | bytes 589832 | tf_op jit(solution)/shard_map/ppermute | solution.py:101
  112.6 2.9 %collective-permute-done.18.right_ref = bf16[32,4096]{1,0:T(8,128)(2,1)S(1)} collective-permute-done((bf16[32,4096]{1,0:T(8,128)(2,1)S(1)}, bf16[32,4096]{1,0:T(8,128)(2,1)S(1)}, u32[]{:S(2)}, u32[]{:S(2)}) %collective-permute-start.18) | collective-permute-done | bytes 262176 | tf_op jit(solution)/shard_map/ppermute | solution.py:101
  121.5 2.9 %collective-permute-start.24 = (bf16[32,4096]{1,0:T(8,128)(2,1)S(1)}, bf16[32,4096]{1,0:T(8,128)(2,1)S(1)}, u32[]{:S(2)}, u32[]{:S(2)}) collective-permute-start(bf16[32,4096]{1,0:T(8,128)(2,1)S(1)} %apply_layer.22), channel_id=1, source_target_pairs={{1,4},{2,5},{3,6},{5,8},{6,9},{7,10},{9,12},{10,13},{11,14},{13,16... | collective-permute-start | bytes 786440 | tf_op jit(solution)/shard_map/ppermute | solution.py:101
  127.0 2.3 %collective-permute-start.37 = (bf16[24,4096]{1,0:T(8,128)(2,1)S(1)}, bf16[24,4096]{1,0:T(8,128)(2,1)S(1)}, u32[]{:S(2)}, u32[]{:S(2)}) collective-permute-start(bf16[24,4096]{1,0:T(8,128)(2,1)S(1)} %apply_layer.27), channel_id=1, source_target_pairs={{0,5},{1,6},{2,7},{4,9},{5,10},{6,11},{8,13},{9,14},{10,15},{12,17... | collective-permute-start | bytes 589832 | tf_op jit(solution)/shard_map/ppermute | solution.py:101
  131.3 2.5 %collective-permute-start.39 = (bf16[24,4096]{1,0:T(8,128)(2,1)S(1)}, bf16[24,4096]{1,0:T(8,128)(2,1)S(1)}, u32[]{:S(2)}, u32[]{:S(2)}) collective-permute-start(bf16[24,4096]{1,0:T(8,128)(2,1)S(1)} %apply_layer.27), channel_id=1, source_target_pairs={{1,4},{2,5},{3,6},{5,8},{6,9},{7,10},{9,12},{10,13},{11,14},{13,16... | collective-permute-start | bytes 589832 | tf_op jit(solution)/shard_map/ppermute | solution.py:101
  141.2 2.9 %collective-permute-start.30 = (bf16[32,4096]{1,0:T(8,128)(2,1)S(1)}, bf16[32,4096]{1,0:T(8,128)(2,1)S(1)}, u32[]{:S(2)}, u32[]{:S(2)}) collective-permute-start(bf16[32,4096]{1,0:T(8,128)(2,1)S(1)} %apply_layer.24), channel_id=1, source_target_pairs={{1,4},{2,5},{3,6},{5,8},{6,9},{7,10},{9,12},{10,13},{11,14},{13,16... | collective-permute-start | bytes 786440 | tf_op jit(solution)/shard_map/ppermute | solution.py:101
  146.2 2.8 %collective-permute-start.43 = (bf16[24,4096]{1,0:T(8,128)(2,1)S(1)}, bf16[24,4096]{1,0:T(8,128)(2,1)S(1)}, u32[]{:S(2)}, u32[]{:S(2)}) collective-permute-start(bf16[24,4096]{1,0:T(8,128)(2,1)S(1)} %apply_layer.29), channel_id=1, source_target_pairs={{0,5},{1,6},{2,7},{4,9},{5,10},{6,11},{8,13},{9,14},{10,15},{12,17... | collective-permute-start | bytes 589832 | tf_op jit(solution)/shard_map/ppermute | solution.py:101
  150.9 2.5 %collective-permute-start.45 = (bf16[24,4096]{1,0:T(8,128)(2,1)S(1)}, bf16[24,4096]{1,0:T(8,128)(2,1)S(1)}, u32[]{:S(2)}, u32[]{:S(2)}) collective-permute-start(bf16[24,4096]{1,0:T(8,128)(2,1)S(1)} %apply_layer.29), channel_id=1, source_target_pairs={{1,4},{2,5},{3,6},{5,8},{6,9},{7,10},{9,12},{10,13},{11,14},{13,16... | collective-permute-start | bytes 589832 | tf_op jit(solution)/shard_map/ppermute | solution.py:101
  160.8 2.9 %collective-permute-start.36 = (bf16[32,4096]{1,0:T(8,128)(2,1)S(1)}, bf16[32,4096]{1,0:T(8,128)(2,1)S(1)}, u32[]{:S(2)}, u32[]{:S(2)}) collective-permute-start(bf16[32,4096]{1,0:T(8,128)(2,1)S(1)} %apply_layer.26), channel_id=1, source_target_pairs={{1,4},{2,5},{3,6},{5,8},{6,9},{7,10},{9,12},{10,13},{11,14},{13,16... | collective-permute-start | bytes 786440 | tf_op jit(solution)/shard_map/ppermute | solution.py:101
  167.4 5.0 %collective-permute-done.36.right_ref = bf16[32,4096]{1,0:T(8,128)(2,1)S(1)} collective-permute-done((bf16[32,4096]{1,0:T(8,128)(2,1)S(1)}, bf16[32,4096]{1,0:T(8,128)(2,1)S(1)}, u32[]{:S(2)}, u32[]{:S(2)}) %collective-permute-start.36) | collective-permute-done | bytes 262176 | tf_op jit(solution)/shard_map/ppermute | solution.py:101
  178.3 2.9 %collective-permute-start.42 = (bf16[32,4096]{1,0:T(8,128)(2,1)S(1)}, bf16[32,4096]{1,0:T(8,128)(2,1)S(1)}, u32[]{:S(2)}, u32[]{:S(2)}) collective-permute-start(bf16[32,4096]{1,0:T(8,128)(2,1)S(1)} %apply_layer.28), channel_id=1, source_target_pairs={{1,4},{2,5},{3,6},{5,8},{6,9},{7,10},{9,12},{10,13},{11,14},{13,16... | collective-permute-start | bytes 786440 | tf_op jit(solution)/shard_map/ppermute | solution.py:101
  181.3 3.3 %collective-permute-done.40.left_ref = bf16[32,4096]{1,0:T(8,128)(2,1)S(1)} collective-permute-done((bf16[32,4096]{1,0:T(8,128)(2,1)S(1)}, bf16[32,4096]{1,0:T(8,128)(2,1)S(1)}, u32[]{:S(2)}, u32[]{:S(2)}) %collective-permute-start.40) | collective-permute-done | bytes 262176 | tf_op jit(solution)/shard_map/ppermute | solution.py:101
  184.6 5.1 %collective-permute-done.42.right_ref = bf16[32,4096]{1,0:T(8,128)(2,1)S(1)} collective-permute-done((bf16[32,4096]{1,0:T(8,128)(2,1)S(1)}, bf16[32,4096]{1,0:T(8,128)(2,1)S(1)}, u32[]{:S(2)}, u32[]{:S(2)}) %collective-permute-start.42) | collective-permute-done | bytes 262176 | tf_op jit(solution)/shard_map/ppermute | solution.py:101
  (100 shorter events, 90.3 us)
Async XLA Ops:
  1.0 35.8 %collective-permute-start = (bf16[32,4096]{1,0:T(8,128)(2,1)S(1)}, bf16[32,4096]{1,0:T(8,128)(2,1)S(1)}, u32[]{:S(2)}, u32[]{:S(2)}) collective-permute-start(bf16[32,4096]{1,0:T(8,128)(2,1)S(1)} %slice_bitcast_fusion.8.own_ref), channel_id=1, source_target_pairs={{0,1},{1,2},{2,3},{4,5},{5,6},{6,7},{8,9},{9,10},{10,11},{12,13},{... | collective-permute-start | bytes 786440 | tf_op jit(solution)/shard_map/ppermute | solution.py:101
  4.1 32.7 %collective-permute-start.1 = (bf16[32,4096]{1,0:T(8,128)(2,1)S(1)}, bf16[32,4096]{1,0:T(8,128)(2,1)S(1)}, u32[]{:S(2)}, u32[]{:S(2)}) collective-permute-start(bf16[32,4096]{1,0:T(8,128)(2,1)S(1)} %slice_bitcast_fusion.8.own_ref), channel_id=1, source_target_pairs={{1,0},{2,1},{3,2},{5,4},{6,5},{7,6},{9,8},{10,9},{11,10},{13,12},{... | collective-permute-start | bytes 786440 | tf_op jit(solution)/shard_map/ppermute | solution.py:101
  7.2 16.0 %collective-permute-start.2 = (bf16[24,4096]{1,0:T(8,128)(2,1)S(1)}, bf16[24,4096]{1,0:T(8,128)(2,1)S(1)}, u32[]{:S(2)}, u32[]{:S(2)}) collective-permute-start(bf16[24,4096]{1,0:T(8,128)(2,1)S(1)} %slice_bitcast_fusion.17.own_ref), channel_id=1, source_target_pairs={{0,1},{1,2},{2,3},{4,5},{5,6},{6,7},{8,9},{9,10},{10,11},{12,13},{... | collective-permute-start | bytes 589832 | tf_op jit(solution)/shard_map/ppermute | solution.py:101
  11.2 13.8 %collective-permute-start.3 = (bf16[24,4096]{1,0:T(8,128)(2,1)S(1)}, bf16[24,4096]{1,0:T(8,128)(2,1)S(1)}, u32[]{:S(2)}, u32[]{:S(2)}) collective-permute-start(bf16[24,4096]{1,0:T(8,128)(2,1)S(1)} %slice_bitcast_fusion.17.own_ref), channel_id=1, source_target_pairs={{1,0},{2,1},{3,2},{5,4},{6,5},{7,6},{9,8},{10,9},{11,10},{13,12},{... | collective-permute-start | bytes 589832 | tf_op jit(solution)/shard_map/ppermute | solution.py:101
  29.9 19.4 %collective-permute-start.7 = (bf16[24,4096]{1,0:T(8,128)(2,1)S(1)}, bf16[24,4096]{1,0:T(8,128)(2,1)S(1)}, u32[]{:S(2)}, u32[]{:S(2)}) collective-permute-start(bf16[24,4096]{1,0:T(8,128)(2,1)S(1)} %apply_layer.17), channel_id=1, source_target_pairs={{0,5},{1,6},{2,7},{4,9},{5,10},{6,11},{8,13},{9,14},{10,15},{12,17... | collective-permute-start | bytes 589832 | tf_op jit(solution)/shard_map/ppermute | solution.py:101
  38.8 20.8 %collective-permute-start.4 = (bf16[32,4096]{1,0:T(8,128)(2,1)S(1)}, bf16[32,4096]{1,0:T(8,128)(2,1)S(1)}, u32[]{:S(2)}, u32[]{:S(2)}) collective-permute-start(bf16[32,4096]{1,0:T(8,128)(2,1)S(1)} %apply_layer.16), channel_id=1, source_target_pairs={{0,5},{1,6},{2,7},{4,9},{5,10},{6,11},{8,13},{9,14},{10,15},{12,17... | collective-permute-start | bytes 786440 | tf_op jit(solution)/shard_map/ppermute | solution.py:101
  47.4 15.9 %collective-permute-start.5 = (bf16[32,4096]{1,0:T(8,128)(2,1)S(1)}, bf16[32,4096]{1,0:T(8,128)(2,1)S(1)}, u32[]{:S(2)}, u32[]{:S(2)}) collective-permute-start(bf16[32,4096]{1,0:T(8,128)(2,1)S(1)} %apply_layer.16), channel_id=1, source_target_pairs={{0,4},{1,5},{2,6},{3,7},{4,8},{5,9},{6,10},{7,11},{8,12},{9,13},{1... | collective-permute-start | bytes 786440 | tf_op jit(solution)/shard_map/ppermute | solution.py:101
  49.3 14.0 %collective-permute-start.6 = (bf16[32,4096]{1,0:T(8,128)(2,1)S(1)}, bf16[32,4096]{1,0:T(8,128)(2,1)S(1)}, u32[]{:S(2)}, u32[]{:S(2)}) collective-permute-start(bf16[32,4096]{1,0:T(8,128)(2,1)S(1)} %apply_layer.16), channel_id=1, source_target_pairs={{1,4},{2,5},{3,6},{5,8},{6,9},{7,10},{9,12},{10,13},{11,14},{13,16... | collective-permute-start | bytes 786440 | tf_op jit(solution)/shard_map/ppermute | solution.py:101
  55.5 12.8 %collective-permute-start.13 = (bf16[24,4096]{1,0:T(8,128)(2,1)S(1)}, bf16[24,4096]{1,0:T(8,128)(2,1)S(1)}, u32[]{:S(2)}, u32[]{:S(2)}) collective-permute-start(bf16[24,4096]{1,0:T(8,128)(2,1)S(1)} %apply_layer.19), channel_id=1, source_target_pairs={{0,5},{1,6},{2,7},{4,9},{5,10},{6,11},{8,13},{9,14},{10,15},{12,17... | collective-permute-start | bytes 589832 | tf_op jit(solution)/shard_map/ppermute | solution.py:101
  65.4 26.1 %collective-permute-start.10 = (bf16[32,4096]{1,0:T(8,128)(2,1)S(1)}, bf16[32,4096]{1,0:T(8,128)(2,1)S(1)}, u32[]{:S(2)}, u32[]{:S(2)}) collective-permute-start(bf16[32,4096]{1,0:T(8,128)(2,1)S(1)} %apply_layer.18), channel_id=1, source_target_pairs={{0,5},{1,6},{2,7},{4,9},{5,10},{6,11},{8,13},{9,14},{10,15},{12,17... | collective-permute-start | bytes 786440 | tf_op jit(solution)/shard_map/ppermute | solution.py:101
  79.2 16.0 %collective-permute-start.11 = (bf16[32,4096]{1,0:T(8,128)(2,1)S(1)}, bf16[32,4096]{1,0:T(8,128)(2,1)S(1)}, u32[]{:S(2)}, u32[]{:S(2)}) collective-permute-start(bf16[32,4096]{1,0:T(8,128)(2,1)S(1)} %apply_layer.18), channel_id=1, source_target_pairs={{0,4},{1,5},{2,6},{3,7},{4,8},{5,9},{6,10},{7,11},{8,12},{9,13},{1... | collective-permute-start | bytes 786440 | tf_op jit(solution)/shard_map/ppermute | solution.py:101
  81.1 14.0 %collective-permute-start.12 = (bf16[32,4096]{1,0:T(8,128)(2,1)S(1)}, bf16[32,4096]{1,0:T(8,128)(2,1)S(1)}, u32[]{:S(2)}, u32[]{:S(2)}) collective-permute-start(bf16[32,4096]{1,0:T(8,128)(2,1)S(1)} %apply_layer.18), channel_id=1, source_target_pairs={{1,4},{2,5},{3,6},{5,8},{6,9},{7,10},{9,12},{10,13},{11,14},{13,16... | collective-permute-start | bytes 786440 | tf_op jit(solution)/shard_map/ppermute | solution.py:101
  87.7 14.4 %collective-permute-start.25 = (bf16[24,4096]{1,0:T(8,128)(2,1)S(1)}, bf16[24,4096]{1,0:T(8,128)(2,1)S(1)}, u32[]{:S(2)}, u32[]{:S(2)}) collective-permute-start(bf16[24,4096]{1,0:T(8,128)(2,1)S(1)} %apply_layer.23), channel_id=1, source_target_pairs={{0,5},{1,6},{2,7},{4,9},{5,10},{6,11},{8,13},{9,14},{10,15},{12,17... | collective-permute-start | bytes 589832 | tf_op jit(solution)/shard_map/ppermute | solution.py:101
  89.6 14.4 %collective-permute-start.26 = (bf16[24,4096]{1,0:T(8,128)(2,1)S(1)}, bf16[24,4096]{1,0:T(8,128)(2,1)S(1)}, u32[]{:S(2)}, u32[]{:S(2)}) collective-permute-start(bf16[24,4096]{1,0:T(8,128)(2,1)S(1)} %apply_layer.23), channel_id=1, source_target_pairs={{0,4},{1,5},{2,6},{3,7},{4,8},{5,9},{6,10},{7,11},{8,12},{9,13},{1... | collective-permute-start | bytes 589832 | tf_op jit(solution)/shard_map/ppermute | solution.py:101
  97.3 13.4 %collective-permute-start.16 = (bf16[32,4096]{1,0:T(8,128)(2,1)S(1)}, bf16[32,4096]{1,0:T(8,128)(2,1)S(1)}, u32[]{:S(2)}, u32[]{:S(2)}) collective-permute-start(bf16[32,4096]{1,0:T(8,128)(2,1)S(1)} %apply_layer.20), channel_id=1, source_target_pairs={{0,5},{1,6},{2,7},{4,9},{5,10},{6,11},{8,13},{9,14},{10,15},{12,17... | collective-permute-start | bytes 786440 | tf_op jit(solution)/shard_map/ppermute | solution.py:101
  100.1 12.5 %collective-permute-start.17 = (bf16[32,4096]{1,0:T(8,128)(2,1)S(1)}, bf16[32,4096]{1,0:T(8,128)(2,1)S(1)}, u32[]{:S(2)}, u32[]{:S(2)}) collective-permute-start(bf16[32,4096]{1,0:T(8,128)(2,1)S(1)} %apply_layer.20), channel_id=1, source_target_pairs={{0,4},{1,5},{2,6},{3,7},{4,8},{5,9},{6,10},{7,11},{8,12},{9,13},{1... | collective-permute-start | bytes 786440 | tf_op jit(solution)/shard_map/ppermute | solution.py:101
  102.0 13.5 %collective-permute-start.18 = (bf16[32,4096]{1,0:T(8,128)(2,1)S(1)}, bf16[32,4096]{1,0:T(8,128)(2,1)S(1)}, u32[]{:S(2)}, u32[]{:S(2)}) collective-permute-start(bf16[32,4096]{1,0:T(8,128)(2,1)S(1)} %apply_layer.20), channel_id=1, source_target_pairs={{1,4},{2,5},{3,6},{5,8},{6,9},{7,10},{9,12},{10,13},{11,14},{13,16... | collective-permute-start | bytes 786440 | tf_op jit(solution)/shard_map/ppermute | solution.py:101
  106.0 15.4 %collective-permute-start.31 = (bf16[24,4096]{1,0:T(8,128)(2,1)S(1)}, bf16[24,4096]{1,0:T(8,128)(2,1)S(1)}, u32[]{:S(2)}, u32[]{:S(2)}) collective-permute-start(bf16[24,4096]{1,0:T(8,128)(2,1)S(1)} %apply_layer.25), channel_id=1, source_target_pairs={{0,5},{1,6},{2,7},{4,9},{5,10},{6,11},{8,13},{9,14},{10,15},{12,17... | collective-permute-start | bytes 589832 | tf_op jit(solution)/shard_map/ppermute | solution.py:101
  108.7 15.7 %collective-permute-start.32 = (bf16[24,4096]{1,0:T(8,128)(2,1)S(1)}, bf16[24,4096]{1,0:T(8,128)(2,1)S(1)}, u32[]{:S(2)}, u32[]{:S(2)}) collective-permute-start(bf16[24,4096]{1,0:T(8,128)(2,1)S(1)} %apply_layer.25), channel_id=1, source_target_pairs={{0,4},{1,5},{2,6},{3,7},{4,8},{5,9},{6,10},{7,11},{8,12},{9,13},{1... | collective-permute-start | bytes 589832 | tf_op jit(solution)/shard_map/ppermute | solution.py:101
  110.7 14.3 %collective-permute-start.33 = (bf16[24,4096]{1,0:T(8,128)(2,1)S(1)}, bf16[24,4096]{1,0:T(8,128)(2,1)S(1)}, u32[]{:S(2)}, u32[]{:S(2)}) collective-permute-start(bf16[24,4096]{1,0:T(8,128)(2,1)S(1)} %apply_layer.25), channel_id=1, source_target_pairs={{1,4},{2,5},{3,6},{5,8},{6,9},{7,10},{9,12},{10,13},{11,14},{13,16... | collective-permute-start | bytes 589832 | tf_op jit(solution)/shard_map/ppermute | solution.py:101
  117.6 13.7 %collective-permute-start.22 = (bf16[32,4096]{1,0:T(8,128)(2,1)S(1)}, bf16[32,4096]{1,0:T(8,128)(2,1)S(1)}, u32[]{:S(2)}, u32[]{:S(2)}) collective-permute-start(bf16[32,4096]{1,0:T(8,128)(2,1)S(1)} %apply_layer.22), channel_id=1, source_target_pairs={{0,5},{1,6},{2,7},{4,9},{5,10},{6,11},{8,13},{9,14},{10,15},{12,17... | collective-permute-start | bytes 786440 | tf_op jit(solution)/shard_map/ppermute | solution.py:101
  119.5 14.3 %collective-permute-start.23 = (bf16[32,4096]{1,0:T(8,128)(2,1)S(1)}, bf16[32,4096]{1,0:T(8,128)(2,1)S(1)}, u32[]{:S(2)}, u32[]{:S(2)}) collective-permute-start(bf16[32,4096]{1,0:T(8,128)(2,1)S(1)} %apply_layer.22), channel_id=1, source_target_pairs={{0,4},{1,5},{2,6},{3,7},{4,8},{5,9},{6,10},{7,11},{8,12},{9,13},{1... | collective-permute-start | bytes 786440 | tf_op jit(solution)/shard_map/ppermute | solution.py:101
  121.5 13.7 %collective-permute-start.24 = (bf16[32,4096]{1,0:T(8,128)(2,1)S(1)}, bf16[32,4096]{1,0:T(8,128)(2,1)S(1)}, u32[]{:S(2)}, u32[]{:S(2)}) collective-permute-start(bf16[32,4096]{1,0:T(8,128)(2,1)S(1)} %apply_layer.22), channel_id=1, source_target_pairs={{1,4},{2,5},{3,6},{5,8},{6,9},{7,10},{9,12},{10,13},{11,14},{13,16... | collective-permute-start | bytes 786440 | tf_op jit(solution)/shard_map/ppermute | solution.py:101
  127.0 14.2 %collective-permute-start.37 = (bf16[24,4096]{1,0:T(8,128)(2,1)S(1)}, bf16[24,4096]{1,0:T(8,128)(2,1)S(1)}, u32[]{:S(2)}, u32[]{:S(2)}) collective-permute-start(bf16[24,4096]{1,0:T(8,128)(2,1)S(1)} %apply_layer.27), channel_id=1, source_target_pairs={{0,5},{1,6},{2,7},{4,9},{5,10},{6,11},{8,13},{9,14},{10,15},{12,17... | collective-permute-start | bytes 589832 | tf_op jit(solution)/shard_map/ppermute | solution.py:101
  129.3 14.8 %collective-permute-start.38 = (bf16[24,4096]{1,0:T(8,128)(2,1)S(1)}, bf16[24,4096]{1,0:T(8,128)(2,1)S(1)}, u32[]{:S(2)}, u32[]{:S(2)}) collective-permute-start(bf16[24,4096]{1,0:T(8,128)(2,1)S(1)} %apply_layer.27), channel_id=1, source_target_pairs={{0,4},{1,5},{2,6},{3,7},{4,8},{5,9},{6,10},{7,11},{8,12},{9,13},{1... | collective-permute-start | bytes 589832 | tf_op jit(solution)/shard_map/ppermute | solution.py:101
  131.3 12.8 %collective-permute-start.39 = (bf16[24,4096]{1,0:T(8,128)(2,1)S(1)}, bf16[24,4096]{1,0:T(8,128)(2,1)S(1)}, u32[]{:S(2)}, u32[]{:S(2)}) collective-permute-start(bf16[24,4096]{1,0:T(8,128)(2,1)S(1)} %apply_layer.27), channel_id=1, source_target_pairs={{1,4},{2,5},{3,6},{5,8},{6,9},{7,10},{9,12},{10,13},{11,14},{13,16... | collective-permute-start | bytes 589832 | tf_op jit(solution)/shard_map/ppermute | solution.py:101
  137.3 13.7 %collective-permute-start.28 = (bf16[32,4096]{1,0:T(8,128)(2,1)S(1)}, bf16[32,4096]{1,0:T(8,128)(2,1)S(1)}, u32[]{:S(2)}, u32[]{:S(2)}) collective-permute-start(bf16[32,4096]{1,0:T(8,128)(2,1)S(1)} %apply_layer.24), channel_id=1, source_target_pairs={{0,5},{1,6},{2,7},{4,9},{5,10},{6,11},{8,13},{9,14},{10,15},{12,17... | collective-permute-start | bytes 786440 | tf_op jit(solution)/shard_map/ppermute | solution.py:101
  139.2 14.3 %collective-permute-start.29 = (bf16[32,4096]{1,0:T(8,128)(2,1)S(1)}, bf16[32,4096]{1,0:T(8,128)(2,1)S(1)}, u32[]{:S(2)}, u32[]{:S(2)}) collective-permute-start(bf16[32,4096]{1,0:T(8,128)(2,1)S(1)} %apply_layer.24), channel_id=1, source_target_pairs={{0,4},{1,5},{2,6},{3,7},{4,8},{5,9},{6,10},{7,11},{8,12},{9,13},{1... | collective-permute-start | bytes 786440 | tf_op jit(solution)/shard_map/ppermute | solution.py:101
  141.2 13.7 %collective-permute-start.30 = (bf16[32,4096]{1,0:T(8,128)(2,1)S(1)}, bf16[32,4096]{1,0:T(8,128)(2,1)S(1)}, u32[]{:S(2)}, u32[]{:S(2)}) collective-permute-start(bf16[32,4096]{1,0:T(8,128)(2,1)S(1)} %apply_layer.24), channel_id=1, source_target_pairs={{1,4},{2,5},{3,6},{5,8},{6,9},{7,10},{9,12},{10,13},{11,14},{13,16... | collective-permute-start | bytes 786440 | tf_op jit(solution)/shard_map/ppermute | solution.py:101
  146.2 14.6 %collective-permute-start.43 = (bf16[24,4096]{1,0:T(8,128)(2,1)S(1)}, bf16[24,4096]{1,0:T(8,128)(2,1)S(1)}, u32[]{:S(2)}, u32[]{:S(2)}) collective-permute-start(bf16[24,4096]{1,0:T(8,128)(2,1)S(1)} %apply_layer.29), channel_id=1, source_target_pairs={{0,5},{1,6},{2,7},{4,9},{5,10},{6,11},{8,13},{9,14},{10,15},{12,17... | collective-permute-start | bytes 589832 | tf_op jit(solution)/shard_map/ppermute | solution.py:101
  149.0 14.7 %collective-permute-start.44 = (bf16[24,4096]{1,0:T(8,128)(2,1)S(1)}, bf16[24,4096]{1,0:T(8,128)(2,1)S(1)}, u32[]{:S(2)}, u32[]{:S(2)}) collective-permute-start(bf16[24,4096]{1,0:T(8,128)(2,1)S(1)} %apply_layer.29), channel_id=1, source_target_pairs={{0,4},{1,5},{2,6},{3,7},{4,8},{5,9},{6,10},{7,11},{8,12},{9,13},{1... | collective-permute-start | bytes 589832 | tf_op jit(solution)/shard_map/ppermute | solution.py:101
  150.9 12.8 %collective-permute-start.45 = (bf16[24,4096]{1,0:T(8,128)(2,1)S(1)}, bf16[24,4096]{1,0:T(8,128)(2,1)S(1)}, u32[]{:S(2)}, u32[]{:S(2)}) collective-permute-start(bf16[24,4096]{1,0:T(8,128)(2,1)S(1)} %apply_layer.29), channel_id=1, source_target_pairs={{1,4},{2,5},{3,6},{5,8},{6,9},{7,10},{9,12},{10,13},{11,14},{13,16... | collective-permute-start | bytes 589832 | tf_op jit(solution)/shard_map/ppermute | solution.py:101
  (18 other events, 166.0 us)
